TPU v7x, 512 devices: a whole 4x8x8 slice. The times are simulated.
512 devices in a mesh: depth: 32 (over y, z_lo), height: 16 (over z_hi, x, core).
Axes of the slice: x: 4, y: 8, z: 8 (z_hi: 2, z_lo: 4; z = z_hi * 4 + z_lo), core: 2. Of those that a mesh axis runs over, the one named last changes fastest.
Arguments:
- volume: float32 [32, 256, 2048], P('height', 'depth'), may hold values from -6 to 6
- measured: float32 [16, 32, 2048], P(None, 'height', 'depth'), may hold values from -12 to 12
- taps: float32 [4, 16, 256], P(None, None, 'depth'), may hold values from 0.01 to 0.1
- band_offset: int32 [16, 32], replicated, may hold values from -64 to 64
- angle_index: int32 [16], replicated, may hold values from 0 to 719
Outputs:
- denoised: float32 [32, 256, 2048], P('height', 'depth')
Inputs may be any that keep to these rules, and one draw needn't show every extreme that they name: `band_offset`: band offsets of every angle and brick lie within plus or minus 64.
All inputs are finite; a program needn't handle non-finite values.
Results may differ from a plain program's by a relative error of at most 0.0003.
Values sent between devices are 32-bit elements; how exact they have to be, the bound alone decides.
A program may use at most 64 MiB of HBM per device.

v0:
```python
import math

import jax
import jax.numpy as jnp
from jax import lax
from jax.sharding import PartitionSpec as P

TAPS = 4
OFFMAX = 64
N_VIEWS = 720
SWEEPS = 2


relax_step = 0.5
tv_step = 0.08
tv_eps = 0.1


def shifted_2(value, axis, by):
    count = lax.axis_size(axis)
    pairs = [(i, i + by) for i in range(count) if 0 <= i + by < count]
    return lax.ppermute(value, axis, pairs)


def cut_along(value, dim, count):
    shape = value.shape
    parts = value.reshape(*shape[:dim], count, shape[dim] // count, *shape[dim + 1 :])
    return jnp.moveaxis(parts, dim, 0)


def sent_and_summed(value, axis, dim):
    count = lax.axis_size(axis)
    parts = lax.all_to_all(cut_along(value, dim, count), axis, 0, 0, tiled=True)
    return jnp.sum(parts, axis=0)


def in_order(parts, dim):
    shape = list(parts.shape[1:])
    shape[dim] *= parts.shape[0]
    return jnp.moveaxis(parts, 0, dim).reshape(shape)


def copy_for_each(value, axis):
    copies = jnp.broadcast_to(value, (lax.axis_size(axis), *value.shape))
    return lax.all_to_all(copies, axis, split_axis=0, concat_axis=0, tiled=True)


def gather_directly(value, axis, dim):
    return in_order(copy_for_each(value, axis), dim)


def with_halo(block, sides, width):
    for axis, dim in sides:
        count = lax.axis_size(axis)
        forward = [(i, i + 1) for i in range(count - 1)]
        backward = [(target, source) for source, target in forward]
        low = lax.ppermute(
            lax.slice_in_dim(block, block.shape[dim] - width, None, axis=dim), axis, forward
        )
        high = lax.ppermute(lax.slice_in_dim(block, 0, width, axis=dim), axis, backward)
        block = jnp.concatenate([low, block, high], axis=dim)
    return block


def cone_weights(taps, angle_index, first_slice, total_slices):
    slices = taps.shape[2]
    angle_value = 2.0 * math.pi / N_VIEWS * angle_index.astype(jnp.float32)
    depth_place = (first_slice + jnp.arange(slices, dtype=jnp.int32)).astype(jnp.float32) + 0.5
    rise = (
        0.5
        + 0.45
        * jnp.sin(angle_value)[:, None]
        * jnp.cos(math.pi / total_slices * depth_place)[None, :]
    )
    return jnp.stack([taps * (1.0 - rise)[None], taps * rise[None]], axis=2)


def binary_shift(values, amount, toward):
    length = values.shape[-1]
    for bit_number in range((2 * OFFMAX).bit_length()):
        stride = 1 << bit_number
        zero_block = jnp.zeros(values.shape[:-1] + (stride,), values.dtype)
        if toward > 0:
            shifted = jnp.concatenate([zero_block, values[..., : length - stride]], axis=-1)
        else:
            shifted = jnp.concatenate([values[..., stride:], zero_block], axis=-1)
        chosen = amount // stride % 2 == 1
        values = jnp.where(chosen, shifted, values)
    return values


def project(block, factor, offsets):
    columns = block.shape[2]
    reach = 2 * OFFMAX
    term = jnp.einsum("kasy,hyx->kashx", factor, block, precision=lax.Precision.HIGHEST)
    padded = jnp.pad(term, ((0, 0), (0, 0), (0, 0), (0, 0), (OFFMAX + TAPS, OFFMAX)))
    window = columns + reach
    summed = padded[0, ..., TAPS : TAPS + window]
    for tap_number in range(1, TAPS):
        summed = summed + padded[tap_number, ..., TAPS - tap_number : TAPS - tap_number + window]
    amount = (offsets + OFFMAX)[:, None, None, None]
    shifted = binary_shift(summed, amount, 1)[..., reach : reach + columns]
    lower = jnp.pad(shifted[:, 0], ((0, 0), (0, 1), (0, 0)))
    upper = jnp.pad(shifted[:, 1], ((0, 0), (1, 0), (0, 0)))
    return lower + upper


def backproject(extended, factor, offsets):
    columns = extended.shape[2]
    layers = extended.shape[1] - 1
    padded = jnp.pad(extended, ((0, 0), (0, 0), (OFFMAX, OFFMAX + TAPS)))
    amount = (offsets + OFFMAX)[:, None, None]
    shifted = binary_shift(padded, amount, -1)
    moved = jnp.stack(
        [shifted[..., tap_number : tap_number + columns] for tap_number in range(TAPS)], axis=0
    )
    stacked = jnp.stack([moved[:, :, :layers], moved[:, :, 1:]], axis=2)
    return jnp.einsum("kasy,kashx->hyx", factor, stacked, precision=lax.Precision.HIGHEST)


def forward(values, dimension, allowed):
    length = values.shape[dimension]
    following = jnp.concatenate(
        [
            lax.slice_in_dim(values, 1, length, axis=dimension),
            lax.slice_in_dim(values, length - 1, length, axis=dimension),
        ],
        axis=dimension,
    )
    return jnp.where(allowed, following - values, 0.0)


def backward(normal, dimension):
    length = normal.shape[dimension]
    before = jnp.concatenate(
        [
            jnp.zeros_like(lax.slice_in_dim(normal, 0, 1, axis=dimension)),
            lax.slice_in_dim(normal, 0, length - 1, axis=dimension),
        ],
        axis=dimension,
    )
    return normal - before


def allowed_mask(positions, total):
    return (positions >= 0) & (positions + 1 < total)


def tv_sweep(
    values, height_place, depth_place, width_place, height_total, depth_total, width_total
):
    along_h = forward(values, 0, allowed_mask(height_place, height_total)[:, None, None])
    along_d = forward(values, 1, allowed_mask(depth_place, depth_total)[None, :, None])
    along_w = forward(values, 2, allowed_mask(width_place, width_total)[None, None, :])
    inverse = 1.0 / jnp.sqrt(
        tv_eps * tv_eps + along_h * along_h + along_d * along_d + along_w * along_w
    )
    diverge = (
        backward(along_h * inverse, 0)
        + backward(along_d * inverse, 1)
        + backward(along_w * inverse, 2)
    )
    return values + tv_step * diverge


def margin_sweep(
    extended, depth_of, height_of, layer_count, slice_count, margin, height_total, depth_total
):
    columns = extended.shape[2]
    height_place = (
        height_of * layer_count - margin + jnp.arange(layer_count + 2 * margin, dtype=jnp.int32)
    )
    depth_place = (
        depth_of * slice_count - margin + jnp.arange(slice_count + 2 * margin, dtype=jnp.int32)
    )
    width_place = jnp.arange(columns, dtype=jnp.int32)
    return tv_sweep(
        extended, height_place, depth_place, width_place, height_total, depth_total, columns
    )


def per_device(volume, measured, taps, band_offset, angle_index):
    layer_count = volume.shape[0]
    slice_count = volume.shape[1]
    depth_of = lax.axis_index("depth")
    height_of = lax.axis_index("height")
    depth_total = slice_count * lax.axis_size("depth")
    height_total = layer_count * lax.axis_size("height")
    factor = cone_weights(taps, angle_index, depth_of * slice_count, depth_total)
    offsets = lax.dynamic_slice_in_dim(band_offset, depth_of, 1, 1)[:, 0]
    partial_value = project(volume, factor, offsets)
    spill = shifted_2(partial_value[:, layer_count], "height", 1)
    own = partial_value[:, :layer_count].at[:, 0].add(spill)
    summed = sent_and_summed(own, "depth", 2)
    residual = measured - summed
    whole = gather_directly(residual, "depth", 2)
    upper = shifted_2(whole[:, 0], "height", -1)
    extended = jnp.concatenate([whole, upper[:, None]], axis=1)
    update = backproject(extended, factor, offsets)
    values = volume + relax_step * update
    widened = with_halo(values, (("depth", 1), ("height", 0)), SWEEPS)
    for sweep_index in range(SWEEPS):
        widened = margin_sweep(
            widened,
            depth_of,
            height_of,
            layer_count,
            slice_count,
            SWEEPS,
            height_total,
            depth_total,
        )
    values = widened[SWEEPS:-SWEEPS, SWEEPS:-SWEEPS]
    return values


def solution(mesh):
    in_specs = (
        P("height", "depth", None),
        P(None, "height", "depth"),
        P(None, None, "depth"),
        P(),
        P(),
    )
    out_specs = P("height", "depth", None)
    return jax.shard_map(
        per_device, mesh=mesh, in_specs=in_specs, out_specs=out_specs, check_vma=False
    )
```

profile of v0, /device:TPU:448, one launch (start us, length us, event | category | flops | bytes accessed | tf_op | source)
XLA Modules:
  0.0 111.4 jit_solution(15659609201911099302)
XLA Ops:
  0.0 0.7 sine_multiply_fusion
  0.7 0.9 add_reduce_fusion
  1.8 0.7 multiply_bitcast_fusion.1
  2.5 2.8 %fusion.27 = f32[4,16,2,2,2048]{4,1,3,2,0:T(8,128)S(1)} fusion(f32[2,8,2048]{2,1,0:T(8,128)} %param.7, f32[4,16,1,8]{1,3,2,0:T(8,128)S(1)} %get-tuple-element.34, f32[4,16,1,8]{1,3,2,0:T(8,128)S(1)} %get-tuple-element.33), kind=kOutput, calls=%fused_computation.82 | convolution fusion | flops 50332672 | bytes 2232320 | tf_op jit(solution)/shard_map/kasy,hyx->kashx/dot_general | solution.py:95
  5.2 0.7 fusion.15
  5.9 0.8 pad_select_fusion.7
  6.7 0.2 pad_select_fusion.6
  6.9 0.2 pad_select_fusion.5
  7.1 0.2 pad_select_fusion.4
  7.4 0.2 pad_select_fusion.3
  7.6 0.2 pad_select_fusion.2
  7.8 0.2 pad_select_fusion.1
  8.1 0.1 pad_select_fusion
  8.3 1.9 %collective-permute-start = (f32[16,2048]{1,0:T(8,128)S(1)}, f32[16,2048]{1,0:T(8,128)S(1)}, u32[]{:S(2)}, u32[]{:S(2)}) collective-permute-start(f32[16,2048]{1,0:T(8,128)S(1)} %fusion.26), channel_id=1, source_target_pairs={{0,1},{1,2},{2,3},{3,4},{4,5},{5,6},{6,7},{7,8},{8,9},{9,10},{10,1... | collective-permute-start | bytes 393224 | tf_op jit(solution)/shard_map/ppermute | solution.py:22
  10.2 10.3 %collective-permute-done = f32[16,2048]{1,0:T(8,128)S(1)} collective-permute-done((f32[16,2048]{1,0:T(8,128)S(1)}, f32[16,2048]{1,0:T(8,128)S(1)}, u32[]{:S(2)}, u32[]{:S(2)}) %collective-permute-start) | collective-permute-done | bytes 131104 | tf_op jit(solution)/shard_map/ppermute | solution.py:22
  20.6 0.2 reshape.894
  20.8 0.3 copy.30
  21.1 0.3 reshape.900
  21.5 20.6 %all_to_all.10 = f32[32,1,2048]{2,1,0:T(1,128)S(1)} all-to-all(f32[32,1,2048]{2,1,0:T(1,128)S(1)} %reshape.900), channel_id=1, replica_groups=mesh['depth'=32,'height'=16] {'depth'}, dimensions={0} | all-to-all | bytes 524288 | tf_op jit(solution)/shard_map/all_to_all | solution.py:33
  42.1 0.5 broadcast.1410
  42.6 1.3 %reduce.4 = f32[32,2048]{1,0:T(8,128)S(1)} reduce(f32[32,1,2048]{2,1,0:T(1,128)S(1)} %all_to_all.10, f32[]{:T(128)} %broadcast.1410), dimensions={1}, to_apply=%all_to_all.6.reduce_sub_computation | reduce | bytes 524292 | tf_op jit(solution)/shard_map/all_to_all | solution.py:33
  43.8 0.2 reshape.901
  44.2 0.3 reshape.902
  44.5 15.1 %all_to_all.11 = f32[32,1,2048]{2,1,0:T(1,128)S(1)} all-to-all(f32[32,1,2048]{2,1,0:T(1,128)S(1)} %reshape.902), channel_id=1, replica_groups=mesh['depth'=32,'height'=16] {'depth'}, dimensions={0} | all-to-all | bytes 524288 | tf_op jit(solution)/shard_map/all_to_all | solution.py:45
  59.6 1.3 %reduce.5 = f32[32,2048]{1,0:T(8,128)S(1)} reduce(f32[32,1,2048]{2,1,0:T(1,128)S(1)} %all_to_all.11, f32[]{:T(128)} %broadcast.1410), dimensions={1}, to_apply=%all_to_all.7.reduce_sub_computation | reduce | bytes 524292 | tf_op jit(solution)/shard_map/all_to_all | solution.py:45
  60.9 0.2 reshape.903
  61.2 0.3 copy.19
  61.5 0.2 reshape.895
  61.7 2.1 %collective-permute-start.1 = (f32[16,2048]{1,0:T(8,128)S(1)}, f32[16,2048]{1,0:T(8,128)S(1)}, u32[]{:S(2)}, u32[]{:S(2)}) collective-permute-start(f32[16,2048]{1,0:T(8,128)S(1)} %slice_bitcast_fusion.8), channel_id=1, source_target_pairs={{1,0},{2,1},{3,2},{4,3},{5,4},{6,5},{7,6},{8,7},{9,8},{10,9},{11,1... | collective-permute-start | bytes 393224 | tf_op jit(solution)/shard_map/ppermute | solution.py:22
  63.8 2.3 %collective-permute-done.1 = f32[16,2048]{1,0:T(8,128)S(1)} collective-permute-done((f32[16,2048]{1,0:T(8,128)S(1)}, f32[16,2048]{1,0:T(8,128)S(1)}, u32[]{:S(2)}, u32[]{:S(2)}) %collective-permute-start.1) | collective-permute-done | bytes 131104 | tf_op jit(solution)/shard_map/ppermute | solution.py:22
  66.1 0.2 select_maximum_fusion
  66.3 0.2 slice.250
  66.5 0.2 pad_select_fusion.15
  66.7 0.2 slice.251
  66.8 0.1 pad_select_fusion.14
  67.0 0.2 slice.252
  67.2 0.2 slice.253
  67.4 0.1 pad_select_fusion.12
  67.5 0.2 slice.254
  67.7 0.1 pad_select_fusion.11
  67.8 0.2 slice.255
  68.0 0.1 pad_select_fusion.10
  68.1 0.2 slice.256
  68.4 0.1 pad_select_fusion.8
  68.6 0.4 slice_bitcast_fusion.5
  68.9 0.2 pad_maximum_fusion
  69.1 0.2 slice_bitcast_fusion.1
  69.3 0.7 copy-done
  70.0 1.2 %fusion.2 = f32[2,8,2048]{2,1,0:T(8,128)S(1)} fusion(f32[2,8,2048]{2,1,0:T(8,128)S(1)} %copy-done, f32[4,16,1,2,2048]{4,1,2,3,0:T(8,128)S(1)} %get-tuple-element.22, f32[4,16,1,2,2048]{4,1,2,3,0:T(8,128)S(1)} %get-tuple-element.21, f32[4,16,1,8]{1,3,2,0:T(8,128)S(1)} %get-tuple-element.34, f32[4,16,1,8]{1,3,2,0:T(8,128)S(1)} %get-tuple-element.33), kind=kOutput, calls=%fused_computation.7 | convolution fusion | flops 50922496 | bytes 2363392 | tf_op jit(solution)/shard_map/kasy,kashx->hyx/dot_general | solution.py:118
  71.2 4.8 %collective-permute-start.2 = (f32[2,2,2048]{2,1,0:T(2,128)S(1)}, f32[2,2,2048]{2,1,0:T(2,128)S(1)}, u32[]{:S(2)}, u32[]{:S(2)}) collective-permute-start(f32[2,2,2048]{2,1,0:T(2,128)S(1)} %get-tuple-element.31), channel_id=1, source_target_pairs={{0,16},{16,32},{32,48},{48,64},{64,80},{80,96},{96,112},{112,128},... | collective-permute-start | bytes 98312 | tf_op jit(solution)/shard_map/ppermute | solution.py:57
  76.0 1.9 %collective-permute-start.3 = (f32[2,2,2048]{2,1,0:T(2,128)S(1)}, f32[2,2,2048]{2,1,0:T(2,128)S(1)}, u32[]{:S(2)}, u32[]{:S(2)}) collective-permute-start(f32[2,2,2048]{2,1,0:T(2,128)S(1)} %get-tuple-element.32), channel_id=1, source_target_pairs={{16,0},{32,16},{48,32},{64,48},{80,64},{96,80},{112,96},{128,112},... | collective-permute-start | bytes 98312 | tf_op jit(solution)/shard_map/ppermute | solution.py:60
  78.0 6.5 %collective-permute-done.3 = f32[2,2,2048]{2,1,0:T(2,128)S(1)} collective-permute-done((f32[2,2,2048]{2,1,0:T(2,128)S(1)}, f32[2,2,2048]{2,1,0:T(2,128)S(1)}, u32[]{:S(2)}, u32[]{:S(2)}) %collective-permute-start.3) | collective-permute-done | bytes 32800 | tf_op jit(solution)/shard_map/ppermute | solution.py:60
  84.6 8.4 %collective-permute-start.5 = (f32[2,12,2048]{2,1,0:T(8,128)S(1)}, f32[2,12,2048]{2,1,0:T(8,128)S(1)}, u32[]{:S(2)}, u32[]{:S(2)}) collective-permute-start(f32[2,12,2048]{2,1,0:T(8,128)S(1)} %pad_maximum_fusion.2), channel_id=1, source_target_pairs={{1,0},{2,1},{3,2},{4,3},{5,4},{6,5},{7,6},{8,7},{9,8},{10,9},{11,1... | collective-permute-start | bytes 589832 | tf_op jit(solution)/shard_map/ppermute | solution.py:60
  93.0 1.9 %collective-permute-start.4 = (f32[2,12,2048]{2,1,0:T(8,128)S(1)}, f32[2,12,2048]{2,1,0:T(8,128)S(1)}, u32[]{:S(2)}, u32[]{:S(2)}) collective-permute-start(f32[2,12,2048]{2,1,0:T(8,128)S(1)} %pad_maximum_fusion.2), channel_id=1, source_target_pairs={{0,1},{1,2},{2,3},{3,4},{4,5},{5,6},{6,7},{7,8},{8,9},{9,10},{10,1... | collective-permute-start | bytes 589832 | tf_op jit(solution)/shard_map/ppermute | solution.py:57
  94.9 1.9 %collective-permute-done.5 = f32[2,12,2048]{2,1,0:T(8,128)S(1)} collective-permute-done((f32[2,12,2048]{2,1,0:T(8,128)S(1)}, f32[2,12,2048]{2,1,0:T(8,128)S(1)}, u32[]{:S(2)}, u32[]{:S(2)}) %collective-permute-start.5) | collective-permute-done | bytes 196640 | tf_op jit(solution)/shard_map/ppermute | solution.py:60
  96.8 9.8 %collective-permute-done.4 = f32[2,12,2048]{2,1,0:T(8,128)S(1)} collective-permute-done((f32[2,12,2048]{2,1,0:T(8,128)S(1)}, f32[2,12,2048]{2,1,0:T(8,128)S(1)}, u32[]{:S(2)}, u32[]{:S(2)}) %collective-permute-start.4) | collective-permute-done | bytes 196640 | tf_op jit(solution)/shard_map/ppermute | solution.py:57
  107.0 0.3 slice.270
  107.3 0.6 fusion.49
  107.9 0.4 fusion.51
  108.3 0.5 multiply_add_fusion
  109.1 0.3 slice.279
  109.4 0.5 fusion.50
  110.0 0.6 fusion.48
  110.6 0.8 slice_add_fusion
  (38 shorter events, 1.5 us)
Async XLA Ops:
  8.3 12.3 %collective-permute-start = (f32[16,2048]{1,0:T(8,128)S(1)}, f32[16,2048]{1,0:T(8,128)S(1)}, u32[]{:S(2)}, u32[]{:S(2)}) collective-permute-start(f32[16,2048]{1,0:T(8,128)S(1)} %fusion.26), channel_id=1, source_target_pairs={{0,1},{1,2},{2,3},{3,4},{4,5},{5,6},{6,7},{7,8},{8,9},{9,10},{10,1... | collective-permute-start | bytes 393224 | tf_op jit(solution)/shard_map/ppermute | solution.py:22
  20.8 23.3 %copy-start.1 = (f32[16,2,64]{2,1,0:T(2,128)S(1)}, f32[16,2,64]{2,1,0:T(2,128)}, u32[]{:S(2)}) copy-start(f32[16,2,64]{2,1,0:T(2,128)} %param.8) | copy-start | bytes 24580
  61.7 4.4 %collective-permute-start.1 = (f32[16,2048]{1,0:T(8,128)S(1)}, f32[16,2048]{1,0:T(8,128)S(1)}, u32[]{:S(2)}, u32[]{:S(2)}) collective-permute-start(f32[16,2048]{1,0:T(8,128)S(1)} %slice_bitcast_fusion.8), channel_id=1, source_target_pairs={{1,0},{2,1},{3,2},{4,3},{5,4},{6,5},{7,6},{8,7},{9,8},{10,9},{11,1... | collective-permute-start | bytes 393224 | tf_op jit(solution)/shard_map/ppermute | solution.py:22
  69.1 0.9 copy-start
  71.2 6.7 %collective-permute-start.2 = (f32[2,2,2048]{2,1,0:T(2,128)S(1)}, f32[2,2,2048]{2,1,0:T(2,128)S(1)}, u32[]{:S(2)}, u32[]{:S(2)}) collective-permute-start(f32[2,2,2048]{2,1,0:T(2,128)S(1)} %get-tuple-element.31), channel_id=1, source_target_pairs={{0,16},{16,32},{32,48},{48,64},{64,80},{80,96},{96,112},{112,128},... | collective-permute-start | bytes 98312 | tf_op jit(solution)/shard_map/ppermute | solution.py:57
  76.0 8.5 %collective-permute-start.3 = (f32[2,2,2048]{2,1,0:T(2,128)S(1)}, f32[2,2,2048]{2,1,0:T(2,128)S(1)}, u32[]{:S(2)}, u32[]{:S(2)}) collective-permute-start(f32[2,2,2048]{2,1,0:T(2,128)S(1)} %get-tuple-element.32), channel_id=1, source_target_pairs={{16,0},{32,16},{48,32},{64,48},{80,64},{96,80},{112,96},{128,112},... | collective-permute-start | bytes 98312 | tf_op jit(solution)/shard_map/ppermute | solution.py:60
  84.6 12.2 %collective-permute-start.5 = (f32[2,12,2048]{2,1,0:T(8,128)S(1)}, f32[2,12,2048]{2,1,0:T(8,128)S(1)}, u32[]{:S(2)}, u32[]{:S(2)}) collective-permute-start(f32[2,12,2048]{2,1,0:T(8,128)S(1)} %pad_maximum_fusion.2), channel_id=1, source_target_pairs={{1,0},{2,1},{3,2},{4,3},{5,4},{6,5},{7,6},{8,7},{9,8},{10,9},{11,1... | collective-permute-start | bytes 589832 | tf_op jit(solution)/shard_map/ppermute | solution.py:60
  93.0 13.7 %collective-permute-start.4 = (f32[2,12,2048]{2,1,0:T(8,128)S(1)}, f32[2,12,2048]{2,1,0:T(8,128)S(1)}, u32[]{:S(2)}, u32[]{:S(2)}) collective-permute-start(f32[2,12,2048]{2,1,0:T(8,128)S(1)} %pad_maximum_fusion.2), channel_id=1, source_target_pairs={{0,1},{1,2},{2,3},{3,4},{4,5},{5,6},{6,7},{7,8},{8,9},{9,10},{10,1... | collective-permute-start | bytes 589832 | tf_op jit(solution)/shard_map/ppermute | solution.py:57
where the time goes:
time: 112 us; the launch traced here: 111 us
  blocking collectives  35.7 us (32%)
  waiting for transfers between devices  31 us (28%)
  starting transfers between devices  21 us (19%)
  other arithmetic  12.8 us (11%)
  local copies, waits for them, and re-layouts  6.45 us (6%)
  matrix products  3.97 us (4%)
    all_to_all x1, blocking collectives, sent_and_summed(): parts = lax.all_to_all(cut_along(value, dim, count), axis, 0, 0, tiled=True)  20.6 us
    all_to_all x1, blocking collectives, copy_for_each(): return lax.all_to_all(copies, axis, split_axis=0, concat_axis=0, tiled=True)  15.1 us
    ppermute x2, waiting for transfers between devices, shifted_2(): return lax.ppermute(value, axis, pairs)  12.7 us
    ppermute x2, starting transfers between devices, with_halo(): lax.ppermute(lax.slice_in_dim(block, 0, width, axis=dim), axis, backward)  10.3 us
    ppermute x2, waiting for transfers between devices, with_halo(): lax.ppermute(lax.slice_in_dim(block, block.shape[dim] - width, None, axis...  9.84 us
    ppermute x2, waiting for transfers between devices, with_halo(): lax.ppermute(lax.slice_in_dim(block, 0, width, axis=dim), axis, backward)  8.46 us
    ppermute x2, starting transfers between devices, with_halo(): lax.ppermute(lax.slice_in_dim(block, block.shape[dim] - width, None, axis...  6.7 us
    ppermute x2, starting transfers between devices, shifted_2(): return lax.ppermute(value, axis, pairs)  4.02 us
  transfers between devices with their start and end apart: 6, of which 5 were waited for; matrix products, arithmetic and copies ran while one was open for 0% of the time, Pallas kernels for 0%

commit v1 on v0

v1 whole, which is shorter than its diff:
```python
import functools
import math

import jax
import jax.numpy as jnp
from jax import lax
from jax.experimental import pallas as pl
from jax.experimental.pallas import tpu as pltpu
from jax.sharding import PartitionSpec as P

TAPS = 4
OFFMAX = 64
N_VIEWS = 720
LANES = 128

relax_step = 0.5
tv_step = 0.08
tv_eps = 0.1

MESH = pl.DeviceIdType.MESH


def split_bf16(value):
    high = value.astype(jnp.bfloat16)
    low = (value - high.astype(jnp.float32)).astype(jnp.bfloat16)
    return high, low


def roll_left(value, amount):
    return pltpu.roll(value, value.shape[1] - amount, 1)


def shift_rows(value, amount):
    move = amount + OFFMAX
    top = move // OFFMAX
    moved_left = roll_left(value, OFFMAX)
    moved_right = pltpu.roll(value, OFFMAX, 1)
    value = jnp.where(top == 0, moved_right, jnp.where(top == 1, value, moved_left))
    for bit in range(6):
        stride = 1 << bit
        value = jnp.where((move // stride) % 2 == 1, roll_left(value, stride), value)
    return value


def total_variation(fields, after, before, height_of, depth_of, heights, depths):
    slices, columns = fields[0].shape
    row = lax.broadcasted_iota(jnp.int32, (slices, columns), 0)
    lane = lax.broadcasted_iota(jnp.int32, (slices, columns), 1)
    inner = lane < columns - 1
    last_layer = height_of == heights - 1
    open_row = (row < slices - 1) | (depth_of < depths - 1)
    along_h, along_d, along_w = [], [], []
    for i in range(3):
        here = fields[i]
        up = fields[i + 1] - here
        if i == 2:
            up = jnp.where(last_layer, 0.0, up)
        deep = jnp.where(row == slices - 1, after[i], pltpu.roll(here, slices - 1, 0)) - here
        deep = jnp.where(open_row, deep, 0.0)
        wide = jnp.where(inner, roll_left(here, 1) - here, 0.0)
        scale = lax.rsqrt(tv_eps * tv_eps + up * up + deep * deep + wide * wide)
        if i == 0:
            scale = jnp.where(height_of > 0, scale, 0.0)
        along_h.append(up * scale)
        along_d.append(deep * scale)
        along_w.append(wide * scale)
    here = jnp.where(row == 0, before[0], before[1])
    above = jnp.where(row == 0, before[1], before[2])
    ahead = jnp.where(row == 0, fields[1][0:1], fields[2][0:1])
    up = above - here
    up = jnp.where(last_layer & (row == 1), 0.0, up)
    deep = ahead - here
    wide = jnp.where(inner, roll_left(here, 1) - here, 0.0)
    scale = lax.rsqrt(tv_eps * tv_eps + up * up + deep * deep + wide * wide)
    deep_before = jnp.where(depth_of > 0, deep * scale, 0.0)
    results = []
    for i in (1, 2):
        d_before = jnp.where(row == 0, deep_before[i - 1 : i], pltpu.roll(along_d[i], 1, 0))
        w_before = pltpu.roll(along_w[i], 1, 1)
        diverge = (
            (along_h[i] - along_h[i - 1]) + (along_d[i] - d_before) + (along_w[i] - w_before)
        )
        results.append(fields[i] + tv_step * diverge)
    return results


def kernel(
    heights, depths,
    vol_ref, f1_ref, f2_ref, band_ref, off_ref,
    out_ref,
    halo_ref, part_ref, recv_ref, res_ref,
    main_ref, main_low, main_high,
    lo_ref, hi_ref, got_m, got_pm, got_p, got_mp, got_pp,
    main2_ref, main2_low, main2_high,
    lo2_ref, hi2_ref, got2_m, got2_pm, got2_p, got2_mp,
    halo_sem, scatter_sem, gather_sem, edge_sem, edge2_sem,
):
    height_of = lax.axis_index("height")
    depth_of = lax.axis_index("depth")
    above = lax.rem(height_of + 1, heights)
    below = lax.rem(height_of + heights - 1, heights)
    ahead = lax.rem(depth_of + 1, depths)
    behind = lax.rem(depth_of + depths - 1, depths)
    _, slices, columns = vol_ref.shape
    tiles = columns // LANES
    angles = off_ref.shape[0] // 2

    barrier = pltpu.get_barrier_semaphore()

    def greet(step, carry):
        pl.semaphore_signal(
            barrier, inc=1,
            device_id=(lax.rem(depth_of + step, depths), height_of), device_id_type=MESH,
        )
        return carry

    around = (
        (depth_of, above), (depth_of, below),
        (ahead, above), (ahead, below), (behind, above), (behind, below),
    )
    for target in around:
        pl.semaphore_signal(barrier, inc=1, device_id=target, device_id_type=MESH)
    lax.fori_loop(1, depths, greet, 0)
    pl.semaphore_wait(barrier, depths - 1 + len(around))

    halo_copy = pltpu.make_async_remote_copy(
        src_ref=vol_ref.at[1], dst_ref=halo_ref,
        send_sem=halo_sem.at[0], recv_sem=halo_sem.at[1],
        device_id=(depth_of, above), device_id_type=MESH,
    )
    halo_copy.start()

    zeros = jnp.zeros((slices, LANES), jnp.float32)

    def spread(layers):
        wide = [jnp.concatenate([layer, zeros], axis=1) for layer in layers]
        rows = []
        for layer in wide:
            for tap in range(TAPS):
                rows.append(layer if tap == 0 else pltpu.roll(layer, tap, 1))
        high, low = split_bf16(jnp.concatenate(rows, axis=0))
        return jnp.concatenate([high, low], axis=0)

    own = 2 * TAPS * slices
    first = TAPS * slices
    count = 2 * angles
    image = jnp.dot(
        f1_ref[:, 2 * first :], spread([vol_ref[0], vol_ref[1]]),
        preferred_element_type=jnp.float32,
    )
    halo_copy.wait()
    halo = jnp.where(height_of > 0, halo_ref[...], 0.0)
    image = image + jnp.dot(
        f1_ref[:, : 2 * first], spread([halo]), preferred_element_type=jnp.float32
    )
    image = image[:count] + image[count:]
    image = shift_rows(image, -off_ref[...])
    for r in range(2):
        for tile in range(tiles):
            part_ref[r * tiles + tile] = -image[
                r * angles : (r + 1) * angles, tile * LANES : (tile + 1) * LANES
            ]
    for r in range(2):
        place = r * tiles + depth_of // 2
        part_ref[place] = part_ref[place] + band_ref[r]

    def scatter(step, carry):
        peer = lax.rem(depth_of + step, depths)
        pltpu.make_async_remote_copy(
            src_ref=part_ref.at[peer], dst_ref=recv_ref.at[depth_of],
            send_sem=scatter_sem.at[0], recv_sem=scatter_sem.at[1],
            device_id=(peer, height_of), device_id_type=MESH,
        ).start()
        return carry

    lax.fori_loop(1, depths, scatter, 0)
    recv_ref[depth_of] = part_ref[depth_of]

    def all_of(ref, sem):
        some = ref.at[pl.ds(0, depths - 1)]
        pltpu.make_async_copy(some, some, sem).wait()

    all_of(recv_ref, scatter_sem.at[1])
    sums = [recv_ref[i] for i in range(depths)]
    while len(sums) > 1:
        sums = [sums[i] + sums[i + 1] for i in range(0, len(sums), 2)]
    res_ref[depth_of] = sums[0]

    def gather(step, carry):
        peer = lax.rem(depth_of + step, depths)
        pltpu.make_async_remote_copy(
            src_ref=res_ref.at[depth_of], dst_ref=res_ref.at[depth_of],
            send_sem=gather_sem.at[0], recv_sem=gather_sem.at[1],
            device_id=(peer, height_of), device_id_type=MESH,
        ).start()
        return carry

    lax.fori_loop(1, depths, gather, 0)
    all_of(res_ref, gather_sem.at[1])

    zero_tile = jnp.zeros((angles, LANES), jnp.float32)
    residual = jnp.concatenate(
        [
            jnp.concatenate([res_ref[r * tiles + tile] for tile in range(tiles)] + [zero_tile], axis=1)
            for r in range(2)
        ],
        axis=0,
    )
    residual = shift_rows(residual, off_ref[...])
    high, low = split_bf16(residual)
    update = jnp.dot(
        f2_ref[...], jnp.concatenate([high, low, high, low], axis=0),
        preferred_element_type=jnp.float32,
    )
    updates = []
    for layer in range(3):
        total = None
        for tap in range(TAPS):
            start = layer * first + tap * slices
            term = update[start : start + slices]
            if tap:
                term = roll_left(term, tap)
            total = term if total is None else total + term
        updates.append(total[:, :columns])
    part_c = relax_step * updates[0]
    part_a = vol_ref[0] + relax_step * updates[1]
    part_b = vol_ref[1] + relax_step * updates[2]
    main_ref[0] = part_b
    main_ref[1] = part_a
    main_ref[2] = part_c
    lo_ref[0] = part_a[0:1]
    lo_ref[1] = part_b[0:1]
    lo_ref[2] = part_c[0:1]
    last = slices - 1
    hi_ref[0] = part_b[last:]
    hi_ref[1] = part_a[last:]
    hi_ref[2] = part_c[last:]

    def send_all(moves, sems):
        copies = []
        for i, (src, dst, target) in enumerate(moves):
            copy = pltpu.make_async_remote_copy(
                src_ref=src, dst_ref=dst, send_sem=sems.at[2 * i], recv_sem=sems.at[2 * i + 1],
                device_id=target, device_id_type=MESH,
            )
            copy.start()
            copies.append(copy)
        return copies

    copies = send_all(
        (
            (main_ref.at[pl.ds(1, 2)], main_high, (depth_of, below)),
            (main_ref.at[0], main_low, (depth_of, above)),
            (hi_ref.at[pl.ds(0, 2)], got_m, (ahead, height_of)),
            (hi_ref.at[pl.ds(1, 2)], got_pm, (ahead, below)),
            (lo_ref, got_p, (behind, height_of)),
            (lo_ref.at[1], got_mp, (behind, above)),
            (lo_ref.at[2], got_pp, (behind, below)),
        ),
        edge_sem,
    )
    for copy in copies:
        copy.wait()

    def topped(value):
        return jnp.where(height_of < heights - 1, value, 0.0)

    fields = [
        main_low[...] + part_c,
        part_a,
        part_b + topped(main_high[1]),
        main_high[0],
    ]
    after = [got_mp[...] + got_p[2], got_p[0], got_p[1] + topped(got_pp[...])]
    before = [got_m[1], got_m[0] + topped(got_pm[1]), got_pm[0]]
    places = (height_of, depth_of, heights, depths)
    part_a, part_b = total_variation(fields, after, before, *places)

    main2_ref[0] = part_a
    main2_ref[1] = part_b
    lo2_ref[0] = part_a[0:1]
    lo2_ref[1] = part_b[0:1]
    hi2_ref[0] = part_a[last:]
    hi2_ref[1] = part_b[last:]
    copies = send_all(
        (
            (main2_ref.at[0], main2_high, (depth_of, below)),
            (main2_ref.at[1], main2_low, (depth_of, above)),
            (hi2_ref, got2_m, (ahead, height_of)),
            (hi2_ref.at[0], got2_pm, (ahead, below)),
            (lo2_ref, got2_p, (behind, height_of)),
            (lo2_ref.at[1], got2_mp, (behind, above)),
        ),
        edge2_sem,
    )
    for copy in copies:
        copy.wait()
    fields = [main2_low[...], part_a, part_b, main2_high[...]]
    after = [got2_mp[...], got2_p[0], got2_p[1]]
    before = [got2_m[0], got2_m[1], got2_pm[...]]
    part_a, part_b = total_variation(fields, after, before, *places)
    out_ref[0] = part_a
    out_ref[1] = part_b
    all_of(part_ref, scatter_sem.at[0])
    all_of(res_ref, gather_sem.at[0])


def factor_matrix(taps, angle_index, first_slice, total_slices):
    tap_count, angles, slices = taps.shape
    angle_value = 2.0 * math.pi / N_VIEWS * angle_index.astype(jnp.float32)
    depth_place = (first_slice + jnp.arange(slices, dtype=jnp.int32)).astype(jnp.float32) + 0.5
    rise = (
        0.5
        + 0.45
        * jnp.sin(angle_value)[:, None]
        * jnp.cos(math.pi / total_slices * depth_place)[None, :]
    )
    lower = (taps * (1.0 - rise)[None]).transpose(1, 0, 2).reshape(angles, tap_count * slices)
    upper = (taps * rise[None]).transpose(1, 0, 2).reshape(angles, tap_count * slices)
    none = jnp.zeros_like(lower)
    return jnp.concatenate(
        [
            jnp.concatenate([upper, lower, none], axis=1),
            jnp.concatenate([none, upper, lower], axis=1),
        ],
        axis=0,
    )


def per_device(volume, measured, taps, band_offset, angle_index):
    heights = lax.axis_size("height")
    depths = lax.axis_size("depth")
    layers, slices, columns = volume.shape
    angles = measured.shape[0]
    depth_of = lax.axis_index("depth")
    factor = factor_matrix(taps, angle_index, depth_of * slices, slices * depths)
    high, low = split_bf16(factor)
    first = TAPS * slices

    def doubled(part):
        return [part[:, :first], part[:, :first], part[:, first:], part[:, first:]]

    f1 = jnp.concatenate(
        [jnp.concatenate(doubled(high), axis=1), jnp.concatenate(doubled(low), axis=1)], axis=0
    )
    f2 = jnp.concatenate([high, high, low, low], axis=0).T
    band = jnp.swapaxes(measured, 0, 1)
    none = jnp.zeros_like(band)
    odd = depth_of % 2 == 1
    band = jnp.where(
        odd, jnp.concatenate([none, band], axis=2), jnp.concatenate([band, none], axis=2)
    )
    offsets = lax.dynamic_slice_in_dim(band_offset, depth_of, 1, 1)
    offsets = jnp.concatenate([offsets, offsets], axis=0)
    f32 = jnp.float32
    chunks = (depths, angles, LANES)
    main = (slices, columns)
    edge = (1, columns)
    vmem = pltpu.VMEM
    scratch = [
        vmem(main, f32), vmem(chunks, f32), vmem(chunks, f32), vmem(chunks, f32),
        vmem((3, *main), f32), vmem(main, f32), vmem((2, *main), f32),
        vmem((3, *edge), f32), vmem((3, *edge), f32),
        vmem((2, *edge), f32), vmem((2, *edge), f32), vmem((3, *edge), f32),
        vmem(edge, f32), vmem(edge, f32),
        vmem((2, *main), f32), vmem(main, f32), vmem(main, f32),
        vmem((2, *edge), f32), vmem((2, *edge), f32),
        vmem((2, *edge), f32), vmem(edge, f32), vmem((2, *edge), f32), vmem(edge, f32),
        pltpu.SemaphoreType.DMA((2,)),
        pltpu.SemaphoreType.DMA((2,)),
        pltpu.SemaphoreType.DMA((2,)),
        pltpu.SemaphoreType.DMA((14,)),
        pltpu.SemaphoreType.DMA((12,)),
    ]
    return pl.pallas_call(
        functools.partial(kernel, heights, depths),
        out_shape=jax.ShapeDtypeStruct(volume.shape, f32),
        in_specs=[pl.BlockSpec(memory_space=pltpu.VMEM)] * 5,
        out_specs=pl.BlockSpec(memory_space=pltpu.VMEM),
        scratch_shapes=scratch,
        compiler_params=pltpu.CompilerParams(
            collective_id=0, has_side_effects=True, vmem_limit_bytes=32 * 1024 * 1024
        ),
    )(volume, f1, f2, band, offsets)


def solution(mesh):
    in_specs = (
        P("height", "depth", None),
        P(None, "height", "depth"),
        P(None, None, "depth"),
        P(),
        P(),
    )
    out_specs = P("height", "depth", None)
    return jax.shard_map(
        per_device, mesh=mesh, in_specs=in_specs, out_specs=out_specs, check_vma=False
    )
```

time: 112 us -> 62.2 us (0.56)
  the two profiles are of different devices: /device:TPU:448 before, /device:TPU:16 now
where the time goes in v1:
time: 62.2 us; the launch traced here: 61.9 us
  Pallas kernels  56.7 us (91%)
  local copies, waits for them, and re-layouts  4.35 us (7%)
  other arithmetic  0.67 us (1%)
    pallas_call x1, Pallas kernels, per_device(): pl.pallas_call(functools.partial(kernel, heights, depths), out_shape=jax....  56.7 us
    unnamed x15, local copies, waits for them, and re-layouts  2.91 us

profile of v1, /device:TPU:16, one launch (start us, length us, event | category | flops | bytes accessed | tf_op | source)
XLA Modules:
  0.0 61.9 jit_solution(4427672426822003004)
XLA Ops:
  0.0 0.0 copy-start
  0.0 0.0 copy-start.5
  0.1 0.6 %copy-done.5 = s32[16]{0:T(128)S(1)} copy-done((s32[16]{0:T(128)S(1)}, s32[16]{0:T(128)}, u32[]{:S(2)}) %copy-start.5) | copy-done | bytes 88
  0.7 0.1 multiply_add_fusion
  0.8 0.0 copy-done
  0.8 0.1 constant_dynamic-slice_fusion
  0.9 0.0 copy-start.4
  0.9 0.1 copy.50
  1.0 0.1 pad_add_fusion
  1.0 0.1 copy.49.off_ref
  1.1 0.5 copy-done.4
  1.6 0.0 copy-start.3
  1.6 0.1 pad_select_fusion.band_ref
  1.7 0.6 %copy-done.3 = f32[4,16,8]{1,2,0:T(8,128)S(1)} copy-done((f32[4,16,8]{1,2,0:T(8,128)S(1)}, f32[4,16,8]{1,2,0:T(8,128)}, u32[]{:S(2)}) %copy-start.3) | copy-done | bytes 2072
  2.3 0.1 copy.36
  2.4 0.1 copy.37
  2.5 0.1 fusion
  2.5 0.1 maximum_maximum_fusion.1
  2.6 0.1 slice.23
  2.7 0.1 copy.40
  2.8 0.1 copy.41
  2.9 0.0 copy-start.2
  2.9 0.0 copy-start.1
  3.0 0.1 maximum_bitcast_fusion.f2_ref
  3.0 0.1 copy.43
  3.1 0.4 copy-done.2
  3.5 0.0 slice-start
  3.5 0.1 copy.44
  3.6 0.6 %slice-done = bf16[32,32]{0,1:T(8,128)(2,1)S(1)} async-done(((bf16[32,96]{0,1:T(8,128)(2,1)}), bf16[32,32]{0,1:T(8,128)(2,1)S(1)}, s32[]{:S(2)}) %slice-start) | async-done | bytes 2072 | tf_op jit(solution)/shard_map/slice | solution.py:341
  4.3 0.1 copy.42
  4.3 0.1 maximum_maximum_fusion.f1_ref
  4.4 0.0 copy-done.1
  4.4 56.7 %shard_map.55 = f32[2,8,2048]{2,1,0:T(8,128)S(1)} custom-call(f32[2,8,2048]{2,1,0:T(8,128)S(1)} %copy-done.1, bf16[64,192]{1,0:T(8,128)(2,1)S(1)} %maximum_maximum_fusion.f1_ref, bf16[96,128]{1,0:T(8,128)(2,1)S(1)} %maximum_bitcast_fusion.f2_ref, f32[2,16,128]{2,1,0:T(8,128)S(1)} %pad_select_fusion.band_ref, s32[32,1]{1,0:T(8,128)S(1)} %copy.49.off_ref), custom_call_target="tpu_custom_call" | custom-call | tf_op jit(solution)/shard_map/pallas_call | solution.py:375
  61.2 0.7 %copy.54 = f32[2,8,2048]{2,1,0:T(8,128)} copy(f32[2,8,2048]{2,1,0:T(8,128)S(1)} %shard_map.55) | data formatting | bytes 262144
  (7 shorter events, 0.1 us)
Async XLA Ops:
  0.0 0.8 %copy-start = (s32[16,32]{1,0:T(8,128)S(1)}, s32[16,32]{1,0:T(8,128)}, u32[]{:S(2)}) copy-start(s32[16,32]{1,0:T(8,128)} %param.8) | copy-start | bytes 6148
  0.0 0.7 %copy-start.5 = (s32[16]{0:T(128)S(1)}, s32[16]{0:T(128)}, u32[]{:S(2)}) copy-start(s32[16]{0:T(128)} %param.9) | copy-start | bytes 196
  0.9 0.7 %copy-start.4 = (f32[16,2,64]{2,1,0:T(2,128)S(1)}, f32[16,2,64]{2,1,0:T(2,128)}, u32[]{:S(2)}) copy-start(f32[16,2,64]{2,1,0:T(2,128)} %param.6) | copy-start | bytes 24580
  1.6 0.7 %copy-start.3 = (f32[4,16,8]{1,2,0:T(8,128)S(1)}, f32[4,16,8]{1,2,0:T(8,128)}, u32[]{:S(2)}) copy-start(f32[4,16,8]{1,2,0:T(8,128)} %param.7) | copy-start | bytes 6148
  2.9 0.6 copy-start.2
  2.9 1.5 %copy-start.1 = (f32[2,8,2048]{2,1,0:T(8,128)S(1)}, f32[2,8,2048]{2,1,0:T(8,128)}, u32[]{:S(2)}) copy-start(f32[2,8,2048]{2,1,0:T(8,128)} %vol_ref.1) | copy-start | bytes 393220
  3.5 0.7 %slice-start = ((bf16[32,96]{0,1:T(8,128)(2,1)}), bf16[32,32]{0,1:T(8,128)(2,1)S(1)}, s32[]{:S(2)}) async-start(bf16[32,96]{0,1:T(8,128)(2,1)} %copy-done.2), calls=%async_computation | async-start | bytes 16384 | tf_op jit(solution)/shard_map/slice | solution.py:341

commit v2 on v1

v2 whole, which is shorter than its diff:
```python
import functools
import math

import jax
import jax.numpy as jnp
from jax import lax
from jax.experimental import pallas as pl
from jax.experimental.pallas import tpu as pltpu
from jax.sharding import PartitionSpec as P

TAPS = 4
OFFMAX = 64
N_VIEWS = 720
LANES = 128
SUBLANES = 8
NEAR = 4

relax_step = 0.5
tv_step = 0.08
tv_eps = 0.1

MESH = pl.DeviceIdType.MESH


def split_bf16(value):
    high = value.astype(jnp.bfloat16)
    low = (value - high.astype(jnp.float32)).astype(jnp.bfloat16)
    return high, low


def roll_left(value, amount):
    return pltpu.roll(value, value.shape[1] - amount, 1)


def shift_rows(value, amount):
    move = amount + OFFMAX
    top = move // OFFMAX
    moved_left = roll_left(value, OFFMAX)
    moved_right = pltpu.roll(value, OFFMAX, 1)
    value = jnp.where(top == 0, moved_right, jnp.where(top == 1, value, moved_left))
    for bit in range(6):
        stride = 1 << bit
        value = jnp.where((move // stride) % 2 == 1, roll_left(value, stride), value)
    return value


def total_variation(fields, after, before, height_of, depth_of, heights, depths):
    slices, columns = fields[0].shape
    row = lax.broadcasted_iota(jnp.int32, (slices, columns), 0)
    lane = lax.broadcasted_iota(jnp.int32, (slices, columns), 1)
    inner = lane < columns - 1
    last_layer = height_of == heights - 1
    open_row = (row < slices - 1) | (depth_of < depths - 1)
    along_h, along_d, along_w = [], [], []
    for i in range(3):
        here = fields[i]
        up = fields[i + 1] - here
        if i == 2:
            up = jnp.where(last_layer, 0.0, up)
        deep = jnp.where(row == slices - 1, after[i], pltpu.roll(here, slices - 1, 0)) - here
        deep = jnp.where(open_row, deep, 0.0)
        wide = jnp.where(inner, roll_left(here, 1) - here, 0.0)
        scale = lax.rsqrt(tv_eps * tv_eps + up * up + deep * deep + wide * wide)
        across = up * scale
        if i == 0:
            across = jnp.where(height_of > 0, across, 0.0)
        along_h.append(across)
        along_d.append(deep * scale)
        along_w.append(wide * scale)
    here = jnp.where(row == 0, before[0], before[1])
    above = jnp.where(row == 0, before[1], before[2])
    ahead = jnp.where(row == 0, fields[1][0:1], fields[2][0:1])
    up = above - here
    up = jnp.where(last_layer & (row == 1), 0.0, up)
    deep = ahead - here
    wide = jnp.where(inner, roll_left(here, 1) - here, 0.0)
    scale = lax.rsqrt(tv_eps * tv_eps + up * up + deep * deep + wide * wide)
    deep_before = jnp.where(depth_of > 0, deep * scale, 0.0)
    results = []
    for i in (1, 2):
        d_before = jnp.where(row == 0, deep_before[i - 1 : i], pltpu.roll(along_d[i], 1, 0))
        w_before = pltpu.roll(along_w[i], 1, 1)
        diverge = (
            (along_h[i] - along_h[i - 1]) + (along_d[i] - d_before) + (along_w[i] - w_before)
        )
        results.append(fields[i] + tv_step * diverge)
    return results


def kernel(
    heights, depths,
    vol_hbm, meas_hbm, taps_hbm, off_hbm, angle_hbm,
    out_ref,
    vol_ref, meas_ref, taps_ref, off_ref, angle_ref,
    halo_ref, part_0, part_1, got_1a, got_1b, got_0a, got_0b, sum_1, sum_0, res_0, res_1,
    main_ref, main_low, main_high,
    lo_ref, hi_ref, got_m, got_pm, got_p, got_mp, got_pp,
    main2_ref, main2_low, main2_high,
    lo2_ref, hi2_ref, got2_m, got2_pm, got2_p, got2_mp,
    load_sem, halo_sem, ring_sem, edge_sem, edge2_sem,
):
    height_of = lax.axis_index("height")
    depth_of = lax.axis_index("depth")
    above, below = height_of + 1, height_of - 1
    has_above, has_below = height_of < heights - 1, height_of > 0
    ahead = lax.rem(depth_of + 1, depths)
    behind = lax.rem(depth_of + depths - 1, depths)
    far_of, near_of = depth_of // NEAR, depth_of % NEAR
    far_count = depths // NEAR
    _, slices, columns = vol_ref.shape
    tiles = columns // LANES
    angles = off_ref.shape[0]
    taps = taps_ref.shape[0]

    loads = [
        pltpu.make_async_copy(src, dst, load_sem.at[i])
        for i, (src, dst) in enumerate(
            (
                (vol_hbm, vol_ref), (angle_hbm, angle_ref), (taps_hbm, taps_ref),
                (off_hbm, off_ref), (meas_hbm, meas_ref),
            )
        )
    ]
    for load in loads:
        load.start()

    barrier = pltpu.get_barrier_semaphore()

    def greet(depth, height):
        pl.semaphore_signal(barrier, inc=1, device_id=(depth, height), device_id_type=MESH)

    def fars():
        order = sorted(range(1, far_count), key=lambda i: -min(i, far_count - i))
        return [lax.rem(far_of + i, far_count) for i in order]

    def nears():
        return [lax.rem(near_of + i, NEAR) for i in range(1, NEAR)]

    @pl.when(has_above)
    def _():
        for depth in (depth_of, ahead, behind):
            greet(depth, above)

    @pl.when(has_below)
    def _():
        for depth in (depth_of, ahead, behind):
            greet(depth, below)

    for depth in (ahead, behind):
        greet(depth, height_of)
    for far in fars():
        greet(far * NEAR + near_of, height_of)
    for near in nears():
        greet(far_of * NEAR + near, height_of)
    partners = far_count + NEAR + 3 * has_above.astype(jnp.int32) + 3 * has_below.astype(jnp.int32)
    pl.semaphore_wait(barrier, partners)

    halo_copy = pltpu.make_async_remote_copy(
        src_ref=vol_hbm.at[1], dst_ref=halo_ref,
        send_sem=halo_sem.at[0], recv_sem=halo_sem.at[1],
        device_id=(depth_of, above), device_id_type=MESH,
    )

    @pl.when(has_above)
    def _():
        halo_copy.start()

    for load in loads[1:]:
        load.wait()

    row = lax.broadcasted_iota(jnp.int32, (angles, LANES), 0)
    lane = lax.broadcasted_iota(jnp.int32, (angles, LANES), 1)
    view = jnp.zeros((angles, LANES), jnp.float32)
    for i in range(angles):
        view = jnp.where(row == i, angle_ref[i].astype(jnp.float32), view)
    angle_value = 2.0 * math.pi / N_VIEWS * view
    depth_place = (depth_of * slices + lane % slices).astype(jnp.float32) + 0.5
    rise = 0.5 + 0.45 * jnp.sin(angle_value) * jnp.cos(math.pi / (slices * depths) * depth_place)
    weight = jnp.concatenate([taps_ref[tap] for tap in range(taps)], axis=0)
    weight = jnp.concatenate(
        [weight, jnp.zeros((taps * slices, LANES - angles), jnp.float32)], axis=1
    )
    weight = jnp.concatenate(
        [weight, jnp.zeros((LANES - taps * slices, LANES), jnp.float32)], axis=0
    ).T[:angles]
    lower, upper = weight * (1.0 - rise), weight * rise
    first = taps * slices
    lower_1 = pltpu.roll(lower, first, 1)
    upper_1 = pltpu.roll(upper, first, 1)
    own = jnp.concatenate([lower, upper + lower_1], axis=0)
    own = jnp.concatenate(split_bf16(own + pltpu.roll(own, 2 * first, 1)), axis=0)
    from_halo = jnp.concatenate(split_bf16((upper + upper_1)[:, : 2 * first]), axis=0)
    back = jnp.concatenate([upper + lower_1, upper_1 + pltpu.roll(lower, 2 * first, 1)], axis=0)
    back = jnp.concatenate([back] * 4, axis=0).T
    back_high = back.astype(jnp.bfloat16).astype(jnp.float32)
    wide_lane = lax.broadcasted_iota(jnp.int32, back.shape, 1)
    back = jnp.where(wide_lane < LANES // 2, back_high, back - back_high).astype(jnp.bfloat16)
    back = back[: 3 * first]
    off_lane = lax.broadcasted_iota(jnp.int32, off_ref.shape, 1)
    offset = jnp.where(off_lane == depth_of, off_ref[...].astype(jnp.float32), 0.0)
    offset = jnp.sum(offset, axis=1, keepdims=True).astype(jnp.int32)
    band_pad = jnp.zeros((angles, LANES - meas_ref.shape[2]), jnp.float32)
    bands = []
    for r in range(2):
        band = jnp.concatenate([meas_ref[:, r, :], band_pad], axis=1)
        bands.append(jnp.where(depth_of % 2 == 1, pltpu.roll(band, LANES // 2, 1), band))

    zeros = jnp.zeros((slices, LANES), jnp.float32)

    def spread(layers):
        wide = [jnp.concatenate([layer, zeros], axis=1) for layer in layers]
        rows = []
        for layer in wide:
            for tap in range(taps):
                rows.append(layer if tap == 0 else pltpu.roll(layer, tap, 1))
        high, low = split_bf16(jnp.concatenate(rows, axis=0))
        return jnp.concatenate([high, low], axis=0)

    def dot(a, b):
        return jnp.dot(a, b, preferred_element_type=jnp.float32)

    def publish(image, band, ref):
        image = shift_rows(image, -offset)
        halves = angles // SUBLANES
        for tile in range(tiles):
            for half in range(halves):
                ref[tile * halves + half] = -image[
                    half * SUBLANES : (half + 1) * SUBLANES, tile * LANES : (tile + 1) * LANES
                ]
        for half in range(halves):
            place = depth_of // 2 * halves + half
            ref[place] = ref[place] + band[half * SUBLANES : (half + 1) * SUBLANES]

    def send(src, dst, number, depth):
        pltpu.make_async_remote_copy(
            src_ref=src, dst_ref=dst,
            send_sem=ring_sem.at[2 * number], recv_sem=ring_sem.at[2 * number + 1],
            device_id=(depth, height_of), device_id_type=MESH,
        ).start()

    def wait_for(ref, number, received):
        pltpu.make_async_copy(ref, ref, ring_sem.at[2 * number + int(received)]).wait()

    def total(parts):
        while len(parts) > 1:
            parts = [a + b for a, b in zip(parts[::2], parts[1::2])]
        return parts[0]

    loads[0].wait()
    both = dot(own, spread([vol_ref[0], vol_ref[1]]))
    both = both[: 2 * angles] + both[2 * angles :]
    publish(both[angles:], bands[1], part_1)
    for far in fars():
        send(part_1.at[pl.ds(far * NEAR, NEAR)], got_1a.at[far_of], 0, far * NEAR + near_of)
    got_1a[far_of] = part_1[pl.ds(far_of * NEAR, NEAR)]

    @pl.when(has_below)
    def _():
        halo_copy.wait_recv()

    @pl.when(jnp.logical_not(has_below))
    def _():
        halo_ref[...] = jnp.zeros_like(halo_ref)

    spilled = dot(from_halo, spread([halo_ref[...]]))
    publish(both[:angles] + (spilled[:angles] + spilled[angles:]), bands[0], part_0)
    for near in nears():
        send(part_0.at[pl.ds(near * far_count, far_count)], got_0a.at[near_of], 1, far_of * NEAR + near)
    got_0a[near_of] = part_0[pl.ds(near_of * far_count, far_count)]

    wait_for(got_1a.at[pl.ds(0, far_count - 1)], 0, True)
    sum_1[...] = total([got_1a[i] for i in range(far_count)])
    for near in nears():
        send(sum_1.at[near], got_1b.at[near_of], 2, far_of * NEAR + near)
    got_1b[near_of] = sum_1[near_of]

    wait_for(got_0a.at[pl.ds(0, NEAR - 1)], 1, True)
    sum_0[...] = total([got_0a[i] for i in range(NEAR)])
    for far in fars():
        send(sum_0.at[far], got_0b.at[far_of], 3, far * NEAR + near_of)
    got_0b[far_of] = sum_0[far_of]

    wait_for(got_1b.at[pl.ds(0, NEAR - 1)], 2, True)
    mine_1, mine_0 = depth_of, near_of * far_count + far_of
    res_1[mine_1] = total([got_1b[i] for i in range(NEAR)])
    for near in nears():
        send(res_1.at[mine_1], res_1.at[mine_1], 4, far_of * NEAR + near)
    wait_for(got_0b.at[pl.ds(0, far_count - 1)], 3, True)
    res_0[mine_0] = total([got_0b[i] for i in range(far_count)])
    for far in fars():
        send(res_0.at[mine_0], res_0.at[mine_0], 5, far * NEAR + near_of)

    wait_for(res_1.at[pl.ds(0, NEAR - 1)], 4, True)
    block_1 = res_1.at[pl.ds(far_of * NEAR, NEAR)]
    for far in fars():
        send(block_1, block_1, 6, far * NEAR + near_of)
    wait_for(res_0.at[pl.ds(0, far_count - 1)], 5, True)
    block_0 = res_0.at[pl.ds(near_of * far_count, far_count)]
    for near in nears():
        send(block_0, block_0, 7, far_of * NEAR + near)
    wait_for(res_1.at[pl.ds(0, depths - NEAR)], 6, True)
    wait_for(res_0.at[pl.ds(0, depths - far_count)], 7, True)

    def settle():
        wait_for(part_1.at[pl.ds(0, depths - NEAR)], 0, False)
        wait_for(part_0.at[pl.ds(0, depths - far_count)], 1, False)
        wait_for(sum_1.at[pl.ds(0, NEAR - 1)], 2, False)
        wait_for(sum_0.at[pl.ds(0, far_count - 1)], 3, False)
        wait_for(res_1.at[pl.ds(0, NEAR - 1)], 4, False)
        wait_for(res_0.at[pl.ds(0, far_count - 1)], 5, False)
        wait_for(res_1.at[pl.ds(0, depths - NEAR)], 6, False)
        wait_for(res_0.at[pl.ds(0, depths - far_count)], 7, False)

        @pl.when(has_above)
        def _():
            halo_copy.wait_send()

    zero_tile = jnp.zeros((angles, LANES), jnp.float32)

    def image_of(ref):
        columns_of = [
            jnp.concatenate([ref[2 * tile], ref[2 * tile + 1]], axis=0) for tile in range(tiles)
        ]
        high, low = split_bf16(
            shift_rows(jnp.concatenate(columns_of + [zero_tile], axis=1), offset)
        )
        return high, low

    high_1, low_1 = image_of(res_1)
    high_0, low_0 = image_of(res_0)
    update = dot(
        back, jnp.concatenate([high_0, high_1, low_0, low_1] * 2, axis=0)
    )
    updates = []
    for layer in range(3):
        whole = None
        for tap in range(taps):
            start = layer * first + tap * slices
            term = update[start : start + slices]
            if tap:
                term = roll_left(term, tap)
            whole = term if whole is None else whole + term
        updates.append(whole[:, :columns])
    part_c = relax_step * updates[0]
    part_a = vol_ref[0] + relax_step * updates[1]
    part_b = vol_ref[1] + relax_step * updates[2]
    main_ref[0] = part_b
    main_ref[1] = part_a
    main_ref[2] = part_c
    lo_ref[0] = part_a[0:1]
    lo_ref[1] = part_b[0:1]
    lo_ref[2] = part_c[0:1]
    last = slices - 1
    hi_ref[0] = part_b[last:]
    hi_ref[1] = part_a[last:]
    hi_ref[2] = part_c[last:]

    def exchange(moves, sems):
        copies = []

        def when(condition, action):
            if condition is None:
                action()
            else:
                pl.when(condition)(action)

        for i, (src, dst, target, sent, got) in enumerate(moves):
            copy = pltpu.make_async_remote_copy(
                src_ref=src, dst_ref=dst, send_sem=sems.at[2 * i], recv_sem=sems.at[2 * i + 1],
                device_id=target, device_id_type=MESH,
            )
            when(sent, copy.start)
            copies.append((copy, sent, got, dst))
        for copy, sent, got, dst in copies:
            when(sent, copy.wait_send)
            when(got, copy.wait_recv)
            if got is not None:

                @pl.when(jnp.logical_not(got))
                def _():
                    dst[...] = jnp.zeros(dst.shape, jnp.float32)

    exchange(
        (
            (main_ref.at[pl.ds(1, 2)], main_high, (depth_of, below), has_below, has_above),
            (main_ref.at[0], main_low, (depth_of, above), has_above, has_below),
            (hi_ref.at[pl.ds(1, 2)], got_pm, (ahead, below), has_below, has_above),
            (lo_ref.at[2], got_pp, (behind, below), has_below, has_above),
            (lo_ref.at[1], got_mp, (behind, above), has_above, has_below),
            (hi_ref.at[pl.ds(0, 2)], got_m, (ahead, height_of), None, None),
            (lo_ref, got_p, (behind, height_of), None, None),
        ),
        edge_sem,
    )
    fields = [main_low[...] + part_c, part_a, part_b + main_high[1], main_high[0]]
    after = [got_mp[...] + got_p[2], got_p[0], got_p[1] + got_pp[...]]
    before = [got_m[1], got_m[0] + got_pm[1], got_pm[0]]
    places = (height_of, depth_of, heights, depths)
    part_a, part_b = total_variation(fields, after, before, *places)

    main2_ref[0] = part_a
    main2_ref[1] = part_b
    lo2_ref[0] = part_a[0:1]
    lo2_ref[1] = part_b[0:1]
    hi2_ref[0] = part_a[last:]
    hi2_ref[1] = part_b[last:]
    exchange(
        (
            (main2_ref.at[0], main2_high, (depth_of, below), has_below, has_above),
            (main2_ref.at[1], main2_low, (depth_of, above), has_above, has_below),
            (hi2_ref.at[0], got2_pm, (ahead, below), has_below, has_above),
            (lo2_ref.at[1], got2_mp, (behind, above), has_above, has_below),
            (hi2_ref, got2_m, (ahead, height_of), None, None),
            (lo2_ref, got2_p, (behind, height_of), None, None),
        ),
        edge2_sem,
    )
    fields = [main2_low[...], part_a, part_b, main2_high[...]]
    after = [got2_mp[...], got2_p[0], got2_p[1]]
    before = [got2_m[0], got2_m[1], got2_pm[...]]
    part_a, part_b = total_variation(fields, after, before, *places)
    out_ref[0] = part_a
    out_ref[1] = part_b
    settle()


def per_device(volume, measured, taps, band_offset, angle_index):
    heights = lax.axis_size("height")
    depths = lax.axis_size("depth")
    f32 = jnp.float32
    layers, slices, columns = volume.shape
    far = depths // NEAR
    taps = jnp.swapaxes(taps, 1, 2)
    tile = (SUBLANES, LANES)
    main = (slices, columns)
    edge = (1, columns)
    vmem = pltpu.VMEM
    scratch = [
        vmem(volume.shape, f32), vmem(measured.shape, f32), vmem(taps.shape, f32),
        vmem(band_offset.shape, jnp.int32), pltpu.SMEM(angle_index.shape, jnp.int32),
        vmem(main, f32), vmem((depths, *tile), f32), vmem((depths, *tile), f32),
        vmem((far, NEAR, *tile), f32), vmem((NEAR, *tile), f32),
        vmem((NEAR, far, *tile), f32), vmem((far, *tile), f32),
        vmem((NEAR, *tile), f32), vmem((far, *tile), f32),
        vmem((depths, *tile), f32), vmem((depths, *tile), f32),
        vmem((3, *main), f32), vmem(main, f32), vmem((2, *main), f32),
        vmem((3, *edge), f32), vmem((3, *edge), f32),
        vmem((2, *edge), f32), vmem((2, *edge), f32), vmem((3, *edge), f32),
        vmem(edge, f32), vmem(edge, f32),
        vmem((2, *main), f32), vmem(main, f32), vmem(main, f32),
        vmem((2, *edge), f32), vmem((2, *edge), f32),
        vmem((2, *edge), f32), vmem(edge, f32), vmem((2, *edge), f32), vmem(edge, f32),
        pltpu.SemaphoreType.DMA((5,)),
        pltpu.SemaphoreType.DMA((2,)),
        pltpu.SemaphoreType.DMA((16,)),
        pltpu.SemaphoreType.DMA((14,)),
        pltpu.SemaphoreType.DMA((12,)),
    ]
    return pl.pallas_call(
        functools.partial(kernel, heights, depths),
        out_shape=jax.ShapeDtypeStruct(volume.shape, f32),
        in_specs=[pl.BlockSpec(memory_space=pl.ANY)] * 5,
        out_specs=pl.BlockSpec(memory_space=pltpu.VMEM),
        scratch_shapes=scratch,
        compiler_params=pltpu.CompilerParams(
            collective_id=0, has_side_effects=True, vmem_limit_bytes=60 * 1024 * 1024
        ),
    )(volume, measured, taps, band_offset, angle_index)


def solution(mesh):
    in_specs = (
        P("height", "depth", None),
        P(None, "height", "depth"),
        P(None, None, "depth"),
        P(),
        P(),
    )
    out_specs = P("height", "depth", None)
    return jax.shard_map(
        per_device, mesh=mesh, in_specs=in_specs, out_specs=out_specs, check_vma=False
    )
```

time: 62.2 us -> 54.2 us (0.87)
  the two profiles are of different devices: /device:TPU:16 before, /device:TPU:7 now
where the time goes in v2:
time: 54.2 us; the launch traced here: 54.1 us
  Pallas kernels  52.5 us (97%)
  local copies, waits for them, and re-layouts  1.57 us (3%)
    pallas_call x1, Pallas kernels, per_device(): pl.pallas_call(functools.partial(kernel, heights, depths), out_shape=jax....  52.5 us
    unnamed x1, local copies, waits for them, and re-layouts  1.57 us

profile of v2, /device:TPU:7, one launch (start us, length us, event | category | flops | bytes accessed | tf_op | source)
XLA Modules:
  0.0 54.1 jit_solution(18361244484940113319)
XLA Ops:
  0.0 52.5 %shard_map.55 = f32[2,8,2048]{2,1,0:T(8,128)} custom-call(f32[2,8,2048]{2,1,0:T(8,128)} %vol_hbm.1, f32[16,2,64]{2,1,0:T(2,128)} %meas_hbm.1, f32[4,8,16]{2,1,0:T(8,128)} %bitcast.1, s32[16,32]{1,0:T(8,128)} %off_hbm.1, s32[16]{0:T(128)} %angle_hbm.1), custom_call_target="tpu_custom_call" | custom-call | tf_op jit(solution)/shard_map/pallas_call | solution.py:459
  52.5 1.6 %copy.7 = f32[2,8,2048]{2,1,0:T(8,128)} copy(f32[2,8,2048]{2,1,0:T(8,128)} %shard_map.55) | data formatting | bytes 262144

commit v3 on v2

v3 whole, which is shorter than its diff:
```python
import functools
import math

import jax
import jax.numpy as jnp
from jax import lax
from jax.experimental import pallas as pl
from jax.experimental.pallas import tpu as pltpu
from jax.sharding import PartitionSpec as P

TAPS = 4
OFFMAX = 64
N_VIEWS = 720
LANES = 128
SUBLANES = 8
NEAR = 4

relax_step = 0.5
tv_step = 0.08
tv_eps = 0.1

MESH = pl.DeviceIdType.MESH


def split_bf16(value):
    high = value.astype(jnp.bfloat16)
    low = (value - high.astype(jnp.float32)).astype(jnp.bfloat16)
    return high, low


def roll_left(value, amount):
    return pltpu.roll(value, value.shape[1] - amount, 1)


def shift_rows(value, amount):
    move = amount + OFFMAX
    top = move // OFFMAX
    moved_left = roll_left(value, OFFMAX)
    moved_right = pltpu.roll(value, OFFMAX, 1)
    value = jnp.where(top == 0, moved_right, jnp.where(top == 1, value, moved_left))
    for bit in range(6):
        stride = 1 << bit
        value = jnp.where((move // stride) % 2 == 1, roll_left(value, stride), value)
    return value


def total_variation(fields, first_layer, height_total, depth_place, depth_total):
    rows, columns = fields[0].shape
    lane = lax.broadcasted_iota(jnp.int32, (rows, columns), 1)
    inner = lane < columns - 1
    open_row = (depth_place >= 0) & (depth_place + 1 < depth_total)
    results = []
    under = None
    for i in range(len(fields) - 1):
        here = fields[i]
        layer = first_layer + i
        up = fields[i + 1] - here
        up = jnp.where((layer >= 0) & (layer + 1 < height_total), up, 0.0)
        deep = jnp.where(open_row, pltpu.roll(here, rows - 1, 0) - here, 0.0)
        wide = jnp.where(inner, roll_left(here, 1) - here, 0.0)
        scale = lax.rsqrt(tv_eps * tv_eps + up * up + deep * deep + wide * wide)
        up = up * scale
        if i:
            deep = deep * scale
            wide = wide * scale
            diverge = (up - under) + (deep - pltpu.roll(deep, 1, 0)) + (wide - pltpu.roll(wide, 1, 1))
            results.append(here + tv_step * diverge)
        under = up
    return results


def kernel(
    heights, depths,
    vol_hbm, meas_hbm, taps_hbm, off_hbm, angle_hbm,
    out_ref,
    vol_ref, meas_ref, taps_ref, off_ref, angle_ref,
    halo_ref, meas_up, side_ref, taps_ahead, taps_behind,
    part_1, got_1a, sum_1, got_1b, res_1,
    part_0, got_0a, sum_0, got_0b, res_0,
    part_2, got_2a, sum_2, got_2b, res_2,
    up_ref, low_ref, down_ref, high_ref,
    up2_ref, low2_ref, up2_edge, low2_edge,
    load_sem, halo_sem, side_sem, ring_sem, edge_sem,
):
    height_of = lax.axis_index("height")
    depth_of = lax.axis_index("depth")
    above, below = height_of + 1, height_of - 1
    has_above, has_below = height_of < heights - 1, height_of > 0
    ahead = lax.rem(depth_of + 1, depths)
    behind = lax.rem(depth_of + depths - 1, depths)
    far_of, near_of = depth_of // NEAR, depth_of % NEAR
    far_count = depths // NEAR
    _, slices, columns = vol_ref.shape
    tiles = columns // LANES
    angles = off_ref.shape[0]
    taps = taps_ref.shape[0]

    barrier = pltpu.get_barrier_semaphore()

    def greet(depth, height):
        pl.semaphore_signal(barrier, inc=1, device_id=(depth, height), device_id_type=MESH)

    def fars():
        order = sorted(range(1, far_count), key=lambda i: -min(i, far_count - i))
        return [lax.rem(far_of + i, far_count) for i in order]

    def nears():
        return [lax.rem(near_of + i, NEAR) for i in range(1, NEAR)]

    @pl.when(has_below)
    def _():
        greet(depth_of, below)

    @pl.when(has_above)
    def _():
        greet(depth_of, above)

    for far in fars():
        greet(far * NEAR + near_of, height_of)
    for near in nears():
        greet(far_of * NEAR + near, height_of)
    for depth in (ahead, behind):
        greet(depth, height_of)

    loads = [
        pltpu.make_async_copy(src, dst, load_sem.at[i])
        for i, (src, dst) in enumerate(
            (
                (vol_hbm, vol_ref), (angle_hbm, angle_ref), (taps_hbm, taps_ref),
                (off_hbm, off_ref), (meas_hbm, meas_ref),
            )
        )
    ]
    for load in loads:
        load.start()
    partners = far_count + NEAR + has_above.astype(jnp.int32) + has_below.astype(jnp.int32)
    pl.semaphore_wait(barrier, partners)

    def remote(src, dst, sems, number, depth, height):
        return pltpu.make_async_remote_copy(
            src_ref=src, dst_ref=dst,
            send_sem=sems.at[2 * number], recv_sem=sems.at[2 * number + 1],
            device_id=(depth, height), device_id_type=MESH,
        )

    halos = [
        remote(vol_hbm.at[0], halo_ref, halo_sem, 0, depth_of, below),
        remote(meas_hbm, meas_up, halo_sem, 1, depth_of, below),
    ]

    @pl.when(has_below)
    def _():
        for copy in halos:
            copy.start()

    for load in loads[1:]:
        load.wait()

    row = lax.broadcasted_iota(jnp.int32, (angles, LANES), 0)
    lane = lax.broadcasted_iota(jnp.int32, (angles, LANES), 1)
    view = jnp.zeros((angles, LANES), jnp.float32)
    for i in range(angles):
        view = jnp.where(row == i, angle_ref[i].astype(jnp.float32), view)
    swing = 0.45 * jnp.sin(2.0 * math.pi / N_VIEWS * view)
    first = taps * slices

    def weights(ref, depth):
        weight = jnp.concatenate([ref[tap] for tap in range(taps)], axis=0)
        weight = jnp.concatenate([weight, jnp.zeros((first, LANES - angles), jnp.float32)], axis=1)
        weight = jnp.concatenate([weight, jnp.zeros((LANES - first, LANES), jnp.float32)], axis=0)
        weight = weight.T[:angles]
        depth_place = (depth * slices + lane % slices).astype(jnp.float32) + 0.5
        rise = 0.5 + swing * jnp.cos(math.pi / (slices * depths) * depth_place)
        return weight * (1.0 - rise), weight * rise

    def offset_of(depth):
        off_lane = lax.broadcasted_iota(jnp.int32, off_ref.shape, 1)
        offset = jnp.where(off_lane == depth, off_ref[...].astype(jnp.float32), 0.0)
        return jnp.sum(offset, axis=1, keepdims=True).astype(jnp.int32)

    def factor(lower, upper):
        return jnp.concatenate(
            [
                upper + pltpu.roll(lower, first, 1),
                pltpu.roll(upper, first, 1) + pltpu.roll(lower, 2 * first, 1),
            ],
            axis=0,
        )

    def transposed(parts):
        whole = jnp.concatenate(parts * 4, axis=0)
        turned = whole.T
        high = turned.astype(jnp.bfloat16).astype(jnp.float32)
        place = lax.broadcasted_iota(jnp.int32, turned.shape, 1)
        return jnp.where(place < turned.shape[1] // 2, high, turned - high).astype(jnp.bfloat16)[: 3 * first]

    lower, upper = weights(taps_ref, depth_of)
    offset = offset_of(depth_of)
    own = jnp.concatenate(
        [upper + pltpu.roll(lower, first, 1), pltpu.roll(upper, first, 1), lower], axis=0
    )
    own = jnp.concatenate(split_bf16(own + pltpu.roll(own, 2 * first, 1)), axis=0)
    from_halo = (lower + pltpu.roll(lower, first, 1))[:, : 2 * first]
    from_halo = jnp.concatenate(split_bf16(from_halo), axis=0)
    band_pad = jnp.zeros((angles, LANES - meas_ref.shape[2]), jnp.float32)

    def band_of(ref, r):
        band = jnp.concatenate([ref[:, r, :], band_pad], axis=1)
        return jnp.where(depth_of % 2 == 1, pltpu.roll(band, LANES // 2, 1), band)

    zeros = jnp.zeros((slices, LANES), jnp.float32)

    def spread(layers):
        wide = [jnp.concatenate([layer, zeros], axis=1) for layer in layers]
        rows = []
        for layer in wide:
            for tap in range(taps):
                rows.append(layer if tap == 0 else pltpu.roll(layer, tap, 1))
        high, low = split_bf16(jnp.concatenate(rows, axis=0))
        return jnp.concatenate([high, low], axis=0)

    def dot(a, b):
        return jnp.dot(a, b, preferred_element_type=jnp.float32)

    halves = angles // SUBLANES

    def publish(image, band, ref):
        image = shift_rows(image, -offset)
        for tile in range(tiles):
            for half in range(halves):
                ref[tile * halves + half] = -image[
                    half * SUBLANES : (half + 1) * SUBLANES, tile * LANES : (tile + 1) * LANES
                ]
        for half in range(halves):
            place = depth_of // 2 * halves + half
            ref[place] = ref[place] + band[half * SUBLANES : (half + 1) * SUBLANES]

    def to_far(src, dst, number):
        for far in fars():
            remote(src(far), dst, ring_sem, number, far * NEAR + near_of, height_of).start()

    def to_near(src, dst, number):
        for near in nears():
            remote(src(near), dst, ring_sem, number, far_of * NEAR + near, height_of).start()

    def wait_for(ref, count, number, received):
        some = ref.at[pl.ds(0, count)]
        pltpu.make_async_copy(some, some, ring_sem.at[2 * number + int(received)]).wait()

    def total(parts):
        while len(parts) > 1:
            parts = [a + b for a, b in zip(parts[::2], parts[1::2])]
        return parts[0]

    class FarFirst:
        def __init__(self, number, part, got_a, summed, got_b, res):
            self.number, self.part, self.got_a = number, part, got_a
            self.summed, self.got_b, self.res = summed, got_b, res

        def one(self):
            to_far(lambda far: self.part.at[pl.ds(far * NEAR, NEAR)], self.got_a.at[far_of], self.number)
            self.got_a[far_of] = self.part[pl.ds(far_of * NEAR, NEAR)]

        def two(self):
            wait_for(self.got_a, far_count - 1, self.number, True)
            self.summed[...] = total([self.got_a[i] for i in range(far_count)])
            to_near(lambda near: self.summed.at[near], self.got_b.at[near_of], self.number + 1)
            self.got_b[near_of] = self.summed[near_of]

        def three(self):
            wait_for(self.got_b, NEAR - 1, self.number + 1, True)
            self.res[depth_of] = total([self.got_b[i] for i in range(NEAR)])
            mine = self.res.at[depth_of]
            to_near(lambda near: mine, mine, self.number + 2)

        def four(self):
            wait_for(self.res, NEAR - 1, self.number + 2, True)
            block = self.res.at[pl.ds(far_of * NEAR, NEAR)]
            to_far(lambda far: block, block, self.number + 3)

        def five(self):
            wait_for(self.res, depths - NEAR, self.number + 3, True)

        def settle(self):
            wait_for(self.part, depths - NEAR, self.number, False)
            wait_for(self.summed, NEAR - 1, self.number + 1, False)
            wait_for(self.res, NEAR - 1, self.number + 2, False)
            wait_for(self.res, depths - NEAR, self.number + 3, False)

    class NearFirst(FarFirst):
        def one(self):
            size = far_count
            to_near(lambda near: self.part.at[pl.ds(near * size, size)], self.got_a.at[near_of], self.number)
            self.got_a[near_of] = self.part[pl.ds(near_of * size, size)]

        def two(self):
            wait_for(self.got_a, NEAR - 1, self.number, True)
            self.summed[...] = total([self.got_a[i] for i in range(NEAR)])
            to_far(lambda far: self.summed.at[far], self.got_b.at[far_of], self.number + 1)
            self.got_b[far_of] = self.summed[far_of]

        def three(self):
            wait_for(self.got_b, far_count - 1, self.number + 1, True)
            place = near_of * far_count + far_of
            self.res[place] = total([self.got_b[i] for i in range(far_count)])
            mine = self.res.at[place]
            to_far(lambda far: mine, mine, self.number + 2)

        def four(self):
            wait_for(self.res, far_count - 1, self.number + 2, True)
            block = self.res.at[pl.ds(near_of * far_count, far_count)]
            to_near(lambda near: block, block, self.number + 3)

        def five(self):
            wait_for(self.res, depths - far_count, self.number + 3, True)

        def settle(self):
            wait_for(self.part, depths - far_count, self.number, False)
            wait_for(self.summed, far_count - 1, self.number + 1, False)
            wait_for(self.res, far_count - 1, self.number + 2, False)
            wait_for(self.res, depths - far_count, self.number + 3, False)

    row_1 = FarFirst(0, part_1, got_1a, sum_1, got_1b, res_1)
    row_2 = NearFirst(4, part_0, got_0a, sum_0, got_0b, res_0)
    row_0 = FarFirst(8, part_2, got_2a, sum_2, got_2b, res_2)
    lowest = jnp.logical_not(has_below)

    loads[0].wait()
    count = 3 * angles
    both = dot(own, spread([vol_ref[0], vol_ref[1]]))
    both = both[:count] + both[count:]
    publish(both[:angles], band_of(meas_ref, 1), part_1)
    row_1.one()

    @pl.when(lowest)
    def _():
        publish(both[2 * angles :], band_of(meas_ref, 0), part_2)
        row_0.one()

    @pl.when(has_above)
    def _():
        for copy in halos:
            copy.wait_recv()
        spilled = dot(from_halo, spread([halo_ref[...]]))
        image = both[angles : 2 * angles] + (spilled[:angles] + spilled[angles:])
        publish(image, band_of(meas_up, 0), part_0)

    @pl.when(jnp.logical_not(has_above))
    def _():
        part_0[...] = jnp.zeros_like(part_0)

    row_2.one()

    last = slices - 2
    sides = [
        remote(taps_hbm, taps_behind, side_sem, 0, ahead, height_of),
        remote(taps_hbm, taps_ahead, side_sem, 1, behind, height_of),
        remote(
            vol_ref.at[:, pl.ds(last, 2)], side_ref.at[:, pl.ds(last, 2)], side_sem, 2, ahead, height_of
        ),
        remote(vol_ref.at[:, pl.ds(0, 2)], side_ref.at[:, pl.ds(0, 2)], side_sem, 3, behind, height_of),
    ]
    for copy in sides:
        copy.start()

    row_1.two()
    pl.when(lowest)(row_0.two)
    row_2.two()
    row_1.three()
    pl.when(lowest)(row_0.three)
    row_2.three()
    for copy in sides:
        copy.wait_recv()
    back = transposed([factor(lower, upper)])
    beyond = []
    for ref, depth, kept in (
        (taps_ahead, ahead, lane % slices < 2),
        (taps_behind, behind, lane % slices >= last),
    ):
        pair = weights(ref, depth)
        beyond.append(factor(*[jnp.where(kept, part, 0.0) for part in pair]))
    beyond = transposed(beyond)
    offset_ahead, offset_behind = offset_of(ahead), offset_of(behind)
    row_1.four()
    pl.when(lowest)(row_0.four)
    row_2.four()
    row_1.five()

    zero_tile = jnp.zeros((angles, LANES), jnp.float32)

    def image_of(ref):
        columns_of = [
            jnp.concatenate([ref[2 * tile], ref[2 * tile + 1]], axis=0) for tile in range(tiles)
        ]
        return jnp.concatenate(columns_of + [zero_tile], axis=1)

    def gathered(update, layer):
        whole = None
        for tap in range(taps):
            start = layer * first + tap * slices
            term = update[start : start + slices]
            if tap:
                term = roll_left(term, tap)
            whole = term if whole is None else whole + term
        return relax_step * whole[:, :columns]

    def backproject(images, layers):
        high, low = zip(*[split_bf16(shift_rows(image, offset)) for image in images])
        update = dot(back, jnp.concatenate([*high, *low] * 2, axis=0))
        shifted = [shift_rows(image, move) for move in (offset_ahead, offset_behind) for image in images]
        high, low = zip(*[split_bf16(image) for image in shifted])
        outer = dot(beyond, jnp.concatenate([*high, *low] * 2, axis=0))
        return [gathered(update, i) for i in layers], [gathered(outer, i) for i in layers]

    side_row = lax.broadcasted_iota(jnp.int32, (slices, columns), 0)
    outside = (side_row < 2) | (side_row >= last)

    def packed(one, two):
        two = jnp.where(side_row < 4, pltpu.roll(two, 2, 0), pltpu.roll(two, slices - 2, 0))
        return jnp.where(outside, one, two)

    def unpacked(value):
        two = jnp.where(side_row < 4, pltpu.roll(value, slices - 2, 0), pltpu.roll(value, 2, 0))
        return value, two

    row_2.five()
    main, side = backproject([image_of(res_1), image_of(res_0)], range(3))
    volume_side = jnp.where(outside, side_ref[...], 0.0)
    layer_0, layer_1 = vol_ref[0] + main[0], vol_ref[1] + main[1]
    side_0, side_1 = volume_side[0] + side[0], volume_side[1] + side[1]
    up_ref[0] = main[2]
    up_ref[1] = layer_1
    up_ref[2] = packed(side[2], side_1)
    down_ref[0] = layer_0
    down_ref[1] = layer_1
    down_ref[2] = packed(side_0, side_1)
    up_copy = remote(up_ref, low_ref, edge_sem, 0, depth_of, above)
    down_copy = remote(down_ref, high_ref, edge_sem, 1, depth_of, below)

    @pl.when(has_above)
    def _():
        up_copy.start()

    @pl.when(has_below)
    def _():
        down_copy.start()

    @pl.when(lowest)
    def _():
        row_0.five()
        image = image_of(res_2)
        low_main, low_side = backproject([jnp.zeros_like(image), image], (2,))
        low_ref[0] = low_main[0]
        low_ref[1] = jnp.zeros((slices, columns), jnp.float32)
        low_ref[2] = packed(low_side[0], jnp.zeros((slices, columns), jnp.float32))

    @pl.when(has_below)
    def _():
        up_copy.wait_recv()

    @pl.when(has_above)
    def _():
        down_copy.wait_recv()

    @pl.when(jnp.logical_not(has_above))
    def _():
        high_ref[...] = jnp.zeros_like(high_ref)

    def joined(inner, outer):
        return jnp.concatenate([inner, outer], axis=0)

    from_low, under = unpacked(low_ref[2])
    over, over_2 = unpacked(high_ref[2])
    fields = [
        joined(low_ref[1], under),
        joined(layer_0 + low_ref[0], side_0 + from_low),
        joined(layer_1, side_1),
        joined(high_ref[0] + main[2], over + side[2]),
        joined(high_ref[1], over_2),
    ]
    place = lax.broadcasted_iota(jnp.int32, fields[0].shape, 0)
    place = depth_of * slices + jnp.where(place < slices + 4, place, place - 2 * slices)
    layers_total, depth_total = 2 * heights, slices * depths
    fields = total_variation(fields, 2 * height_of - 1, layers_total, place, depth_total)

    up2_ref[...] = fields[1][:slices]
    up2_edge[...] = fields[1][slices : slices + 1]
    up_copies = [
        remote(up2_ref, low2_ref, edge_sem, 2, depth_of, above),
        remote(up2_edge, low2_edge, edge_sem, 3, depth_of, above),
    ]

    @pl.when(has_above)
    def _():
        for copy in up_copies:
            copy.start()

    @pl.when(has_below)
    def _():
        for copy in up_copies:
            copy.wait_recv()

    @pl.when(lowest)
    def _():
        low2_ref[...] = jnp.zeros_like(low2_ref)
        low2_edge[...] = jnp.zeros_like(low2_edge)

    edge = jnp.broadcast_to(low2_edge[...], (slices, columns))
    fields = [joined(low2_ref[...], edge), *fields]
    fields = total_variation(fields, 2 * height_of - 1, layers_total, place, depth_total)
    out_ref[0] = fields[0][:slices]
    out_ref[1] = fields[1][:slices]

    row_1.settle()
    row_2.settle()
    pl.when(lowest)(row_0.settle)
    for copy in sides:
        copy.wait_send()

    @pl.when(has_below)
    def _():
        for copy in halos:
            copy.wait_send()
        down_copy.wait_send()

    @pl.when(has_above)
    def _():
        up_copy.wait_send()
        for copy in up_copies:
            copy.wait_send()


def per_device(volume, measured, taps, band_offset, angle_index):
    heights = lax.axis_size("height")
    depths = lax.axis_size("depth")
    f32 = jnp.float32
    layers, slices, columns = volume.shape
    far = depths // NEAR
    taps = jnp.swapaxes(taps, 1, 2)
    tile = (SUBLANES, LANES)
    main = (slices, columns)
    edge = (1, columns)
    vmem = pltpu.VMEM
    far_first = [
        vmem((depths, *tile), f32), vmem((far, NEAR, *tile), f32), vmem((NEAR, *tile), f32),
        vmem((NEAR, *tile), f32), vmem((depths, *tile), f32),
    ]
    near_first = [
        vmem((depths, *tile), f32), vmem((NEAR, far, *tile), f32), vmem((far, *tile), f32),
        vmem((far, *tile), f32), vmem((depths, *tile), f32),
    ]
    scratch = [
        vmem(volume.shape, f32), vmem(measured.shape, f32), vmem(taps.shape, f32),
        vmem(band_offset.shape, jnp.int32), pltpu.SMEM(angle_index.shape, jnp.int32),
        vmem(main, f32), vmem(measured.shape, f32), vmem(volume.shape, f32),
        vmem(taps.shape, f32), vmem(taps.shape, f32),
        *far_first, *near_first, *far_first,
        vmem((3, *main), f32), vmem((3, *main), f32), vmem((3, *main), f32), vmem((3, *main), f32),
        vmem(main, f32), vmem(main, f32), vmem(edge, f32), vmem(edge, f32),
        pltpu.SemaphoreType.DMA((5,)),
        pltpu.SemaphoreType.DMA((4,)),
        pltpu.SemaphoreType.DMA((8,)),
        pltpu.SemaphoreType.DMA((24,)),
        pltpu.SemaphoreType.DMA((8,)),
    ]
    return pl.pallas_call(
        functools.partial(kernel, heights, depths),
        out_shape=jax.ShapeDtypeStruct(volume.shape, f32),
        in_specs=[pl.BlockSpec(memory_space=pl.ANY)] * 5,
        out_specs=pl.BlockSpec(memory_space=pltpu.VMEM),
        scratch_shapes=scratch,
        compiler_params=pltpu.CompilerParams(
            collective_id=0, has_side_effects=True, vmem_limit_bytes=60 * 1024 * 1024
        ),
    )(volume, measured, taps, band_offset, angle_index)


def solution(mesh):
    in_specs = (
        P("height", "depth", None),
        P(None, "height", "depth"),
        P(None, None, "depth"),
        P(),
        P(),
    )
    out_specs = P("height", "depth", None)
    return jax.shard_map(
        per_device, mesh=mesh, in_specs=in_specs, out_specs=out_specs, check_vma=False
    )
```

time: 54.2 us -> 49.6 us (0.915)
  the two profiles are of different devices: /device:TPU:7 before, /device:TPU:320 now
where the time goes in v3:
time: 49.6 us; the launch traced here: 49.4 us
  Pallas kernels  47.8 us (96%)
  local copies, waits for them, and re-layouts  1.57 us (3%)
    pallas_call x1, Pallas kernels, per_device(): pl.pallas_call(functools.partial(kernel, heights, depths), out_shape=jax....  47.8 us
    unnamed x1, local copies, waits for them, and re-layouts  1.57 us

profile of v3, /device:TPU:320, one launch (start us, length us, event | category | flops | bytes accessed | tf_op | source)
XLA Modules:
  0.0 49.4 jit_solution(17733943213298809229)
XLA Ops:
  0.0 47.8 %shard_map.55 = f32[2,8,2048]{2,1,0:T(8,128)} custom-call(f32[2,8,2048]{2,1,0:T(8,128)} %vol_hbm.1, f32[16,2,64]{2,1,0:T(2,128)} %meas_hbm.1, f32[4,8,16]{2,1,0:T(8,128)} %bitcast.1, s32[16,32]{1,0:T(8,128)} %off_hbm.1, s32[16]{0:T(128)} %angle_hbm.1), custom_call_target="tpu_custom_call" | custom-call | tf_op jit(solution)/shard_map/pallas_call | solution.py:566
  47.8 1.6 %copy.7 = f32[2,8,2048]{2,1,0:T(8,128)} copy(f32[2,8,2048]{2,1,0:T(8,128)} %shard_map.55) | data formatting | bytes 262144

commit v4 on v3

--- a/solution.py
+++ b/solution.py
@@ -74,12 +74,12 @@
     vol_hbm, meas_hbm, taps_hbm, off_hbm, angle_hbm,
     out_ref,
     vol_ref, meas_ref, taps_ref, off_ref, angle_ref,
-    halo_ref, meas_up, side_ref, taps_ahead, taps_behind,
+    halo_ref, band_ref, band_up, side_ref, taps_ahead, taps_behind,
     part_1, got_1a, sum_1, got_1b, res_1,
+    part_2, got_2a, sum_2, got_2b, res_2,
     part_0, got_0a, sum_0, got_0b, res_0,
-    part_2, got_2a, sum_2, got_2b, res_2,
     up_ref, low_ref, down_ref, high_ref,
-    up2_ref, low2_ref, up2_edge, low2_edge,
+    up2_ref, low2_ref,
     load_sem, halo_sem, side_sem, ring_sem, edge_sem,
 ):
     height_of = lax.axis_index("height")
@@ -145,16 +145,19 @@
 
     halos = [
         remote(vol_hbm.at[0], halo_ref, halo_sem, 0, depth_of, below),
-        remote(meas_hbm, meas_up, halo_sem, 1, depth_of, below),
-    ]
-
-    @pl.when(has_below)
-    def _():
-        for copy in halos:
-            copy.start()
-
+        remote(band_ref, band_up, halo_sem, 1, depth_of, below),
+    ]
+    pl.when(has_below)(halos[0].start)
     for load in loads[1:]:
         load.wait()
+    band_pad = jnp.zeros((angles, LANES - meas_ref.shape[2]), jnp.float32)
+
+    def band_of(r):
+        band = jnp.concatenate([meas_ref[:, r, :], band_pad], axis=1)
+        return jnp.where(depth_of % 2 == 1, pltpu.roll(band, LANES // 2, 1), band)
+
+    band_ref[...] = band_of(0)
+    pl.when(has_below)(halos[1].start)
 
     row = lax.broadcasted_iota(jnp.int32, (angles, LANES), 0)
     lane = lax.broadcasted_iota(jnp.int32, (angles, LANES), 1)
@@ -202,12 +205,6 @@
     own = jnp.concatenate(split_bf16(own + pltpu.roll(own, 2 * first, 1)), axis=0)
     from_halo = (lower + pltpu.roll(lower, first, 1))[:, : 2 * first]
     from_halo = jnp.concatenate(split_bf16(from_halo), axis=0)
-    band_pad = jnp.zeros((angles, LANES - meas_ref.shape[2]), jnp.float32)
-
-    def band_of(ref, r):
-        band = jnp.concatenate([ref[:, r, :], band_pad], axis=1)
-        return jnp.where(depth_of % 2 == 1, pltpu.roll(band, LANES // 2, 1), band)
-
     zeros = jnp.zeros((slices, LANES), jnp.float32)
 
     def spread(layers):
@@ -252,42 +249,11 @@
             parts = [a + b for a, b in zip(parts[::2], parts[1::2])]
         return parts[0]
 
-    class FarFirst:
+    class NearFirst:
         def __init__(self, number, part, got_a, summed, got_b, res):
             self.number, self.part, self.got_a = number, part, got_a
             self.summed, self.got_b, self.res = summed, got_b, res
 
-        def one(self):
-            to_far(lambda far: self.part.at[pl.ds(far * NEAR, NEAR)], self.got_a.at[far_of], self.number)
-            self.got_a[far_of] = self.part[pl.ds(far_of * NEAR, NEAR)]
-
-        def two(self):
-            wait_for(self.got_a, far_count - 1, self.number, True)
-            self.summed[...] = total([self.got_a[i] for i in range(far_count)])
-            to_near(lambda near: self.summed.at[near], self.got_b.at[near_of], self.number + 1)
-            self.got_b[near_of] = self.summed[near_of]
-
-        def three(self):
-            wait_for(self.got_b, NEAR - 1, self.number + 1, True)
-            self.res[depth_of] = total([self.got_b[i] for i in range(NEAR)])
-            mine = self.res.at[depth_of]
-            to_near(lambda near: mine, mine, self.number + 2)
-
-        def four(self):
-            wait_for(self.res, NEAR - 1, self.number + 2, True)
-            block = self.res.at[pl.ds(far_of * NEAR, NEAR)]
-            to_far(lambda far: block, block, self.number + 3)
-
-        def five(self):
-            wait_for(self.res, depths - NEAR, self.number + 3, True)
-
-        def settle(self):
-            wait_for(self.part, depths - NEAR, self.number, False)
-            wait_for(self.summed, NEAR - 1, self.number + 1, False)
-            wait_for(self.res, NEAR - 1, self.number + 2, False)
-            wait_for(self.res, depths - NEAR, self.number + 3, False)
-
-    class NearFirst(FarFirst):
         def one(self):
             size = far_count
             to_near(lambda near: self.part.at[pl.ds(near * size, size)], self.got_a.at[near_of], self.number)
@@ -320,22 +286,55 @@
             wait_for(self.res, far_count - 1, self.number + 2, False)
             wait_for(self.res, depths - far_count, self.number + 3, False)
 
-    row_1 = FarFirst(0, part_1, got_1a, sum_1, got_1b, res_1)
-    row_2 = NearFirst(4, part_0, got_0a, sum_0, got_0b, res_0)
-    row_0 = FarFirst(8, part_2, got_2a, sum_2, got_2b, res_2)
+    class FarFirst:
+        def __init__(self, number, part, got_a, summed, got_b, res):
+            self.number, self.part, self.got_a = number, part, got_a
+            self.summed, self.got_b, self.res = summed, got_b, res
+
+        def one(self):
+            to_far(lambda far: self.part.at[pl.ds(far * NEAR, NEAR)], self.got_a.at[far_of], self.number)
+            self.got_a[far_of] = self.part[pl.ds(far_of * NEAR, NEAR)]
+
+        def two(self):
+            wait_for(self.got_a, far_count - 1, self.number, True)
+            self.summed[...] = total([self.got_a[i] for i in range(far_count)])
+            to_near(lambda near: self.summed, self.got_b.at[near_of], self.number + 1)
+            self.got_b[near_of] = self.summed[...]
+
+        def three(self):
+            wait_for(self.got_b, NEAR - 1, self.number + 1, True)
+            place = pl.ds(far_of * NEAR, NEAR)
+            self.res[place] = total([self.got_b[i] for i in range(NEAR)])
+            block = self.res.at[place]
+            to_far(lambda far: block, block, self.number + 2)
+
+        def five(self):
+            wait_for(self.res, depths - NEAR, self.number + 2, True)
+
+        def settle(self):
+            wait_for(self.part, depths - NEAR, self.number, False)
+            wait_for(self.got_b, NEAR - 1, self.number + 1, False)
+            wait_for(self.res, depths - NEAR, self.number + 2, False)
+
+    row_1 = NearFirst(0, part_1, got_1a, sum_1, got_1b, res_1)
+    row_2 = FarFirst(4, part_2, got_2a, sum_2, got_2b, res_2)
+    row_0 = FarFirst(7, part_0, got_0a, sum_0, got_0b, res_0)
+    late = height_of == heights // 2 - 1
     lowest = jnp.logical_not(has_below)
 
     loads[0].wait()
     count = 3 * angles
     both = dot(own, spread([vol_ref[0], vol_ref[1]]))
     both = both[:count] + both[count:]
-    publish(both[:angles], band_of(meas_ref, 1), part_1)
+    publish(both[:angles], band_of(1), part_1)
     row_1.one()
 
     @pl.when(lowest)
     def _():
-        publish(both[2 * angles :], band_of(meas_ref, 0), part_2)
+        publish(both[2 * angles :], band_ref[...], part_0)
         row_0.one()
+
+    pl.when(late)(row_1.two)
 
     @pl.when(has_above)
     def _():
@@ -343,11 +342,11 @@
             copy.wait_recv()
         spilled = dot(from_halo, spread([halo_ref[...]]))
         image = both[angles : 2 * angles] + (spilled[:angles] + spilled[angles:])
-        publish(image, band_of(meas_up, 0), part_0)
+        publish(image, band_up[...], part_2)
 
     @pl.when(jnp.logical_not(has_above))
     def _():
-        part_0[...] = jnp.zeros_like(part_0)
+        part_2[...] = jnp.zeros_like(part_2)
 
     row_2.one()
 
@@ -363,12 +362,9 @@
     for copy in sides:
         copy.start()
 
-    row_1.two()
+    pl.when(jnp.logical_not(late))(row_1.two)
     pl.when(lowest)(row_0.two)
     row_2.two()
-    row_1.three()
-    pl.when(lowest)(row_0.three)
-    row_2.three()
     for copy in sides:
         copy.wait_recv()
     back = transposed([factor(lower, upper)])
@@ -381,9 +377,10 @@
         beyond.append(factor(*[jnp.where(kept, part, 0.0) for part in pair]))
     beyond = transposed(beyond)
     offset_ahead, offset_behind = offset_of(ahead), offset_of(behind)
+    row_1.three()
+    pl.when(lowest)(row_0.three)
+    row_2.three()
     row_1.four()
-    pl.when(lowest)(row_0.four)
-    row_2.four()
     row_1.five()
 
     zero_tile = jnp.zeros((angles, LANES), jnp.float32)
@@ -404,12 +401,17 @@
             whole = term if whole is None else whole + term
         return relax_step * whole[:, :columns]
 
-    def backproject(images, layers):
-        high, low = zip(*[split_bf16(shift_rows(image, offset)) for image in images])
-        update = dot(back, jnp.concatenate([*high, *low] * 2, axis=0))
-        shifted = [shift_rows(image, move) for move in (offset_ahead, offset_behind) for image in images]
-        high, low = zip(*[split_bf16(image) for image in shifted])
-        outer = dot(beyond, jnp.concatenate([*high, *low] * 2, axis=0))
+    def prepared(image):
+        moves = (offset, offset_ahead, offset_behind)
+        return [split_bf16(shift_rows(image, move)) for move in moves]
+
+    def backproject(one, two, layers):
+        def stacked(moves):
+            pairs = [image[move] for move in moves for image in (one, two)]
+            return jnp.concatenate([part for side in zip(*pairs) for part in side] * 2, axis=0)
+
+        update = dot(back, stacked((0,)))
+        outer = dot(beyond, stacked((1, 2)))
         return [gathered(update, i) for i in layers], [gathered(outer, i) for i in layers]
 
     side_row = lax.broadcasted_iota(jnp.int32, (slices, columns), 0)
@@ -423,8 +425,9 @@
         two = jnp.where(side_row < 4, pltpu.roll(value, slices - 2, 0), pltpu.roll(value, 2, 0))
         return value, two
 
+    image_1 = prepared(image_of(res_1))
     row_2.five()
-    main, side = backproject([image_of(res_1), image_of(res_0)], range(3))
+    main, side = backproject(image_1, prepared(image_of(res_2)), range(3))
     volume_side = jnp.where(outside, side_ref[...], 0.0)
     layer_0, layer_1 = vol_ref[0] + main[0], vol_ref[1] + main[1]
     side_0, side_1 = volume_side[0] + side[0], volume_side[1] + side[1]
@@ -448,32 +451,53 @@
     @pl.when(lowest)
     def _():
         row_0.five()
-        image = image_of(res_2)
-        low_main, low_side = backproject([jnp.zeros_like(image), image], (2,))
+        image = prepared(image_of(res_0))
+        nothing = [[jnp.zeros_like(part) for part in pair] for pair in image]
+        low_main, low_side = backproject(nothing, image, (2,))
         low_ref[0] = low_main[0]
         low_ref[1] = jnp.zeros((slices, columns), jnp.float32)
         low_ref[2] = packed(low_side[0], jnp.zeros((slices, columns), jnp.float32))
 
+    pl.when(has_below)(up_copy.wait_recv)
+    from_low, under = unpacked(low_ref[2])
+    layer_0 = layer_0 + low_ref[0]
+    side_0 = side_0 + from_low
+    up2_ref[0] = layer_0
+    up2_ref[1] = side_0
+    up_copies = [
+        remote(up2_ref.at[0], low2_ref.at[0], edge_sem, 2, depth_of, above),
+        remote(
+            up2_ref.at[1, pl.ds(0, 2)], low2_ref.at[1, pl.ds(0, 2)], edge_sem, 3, depth_of, above
+        ),
+    ]
+
+    @pl.when(has_above)
+    def _():
+        for copy in up_copies:
+            copy.start()
+        down_copy.wait_recv()
+
+    @pl.when(jnp.logical_not(has_above))
+    def _():
+        high_ref[...] = jnp.zeros_like(high_ref)
+
     @pl.when(has_below)
     def _():
-        up_copy.wait_recv()
-
-    @pl.when(has_above)
-    def _():
-        down_copy.wait_recv()
-
-    @pl.when(jnp.logical_not(has_above))
-    def _():
-        high_ref[...] = jnp.zeros_like(high_ref)
+        for copy in up_copies:
+            copy.wait_recv()
+
+    @pl.when(lowest)
+    def _():
+        low2_ref[...] = jnp.zeros_like(low2_ref)
 
     def joined(inner, outer):
         return jnp.concatenate([inner, outer], axis=0)
 
-    from_low, under = unpacked(low_ref[2])
     over, over_2 = unpacked(high_ref[2])
     fields = [
+        joined(low2_ref[0], jnp.where(side_row < 2, low2_ref[1], 0.0)),
         joined(low_ref[1], under),
-        joined(layer_0 + low_ref[0], side_0 + from_low),
+        joined(layer_0, side_0),
         joined(layer_1, side_1),
         joined(high_ref[0] + main[2], over + side[2]),
         joined(high_ref[1], over_2),
@@ -481,32 +505,7 @@
     place = lax.broadcasted_iota(jnp.int32, fields[0].shape, 0)
     place = depth_of * slices + jnp.where(place < slices + 4, place, place - 2 * slices)
     layers_total, depth_total = 2 * heights, slices * depths
-    fields = total_variation(fields, 2 * height_of - 1, layers_total, place, depth_total)
-
-    up2_ref[...] = fields[1][:slices]
-    up2_edge[...] = fields[1][slices : slices + 1]
-    up_copies = [
-        remote(up2_ref, low2_ref, edge_sem, 2, depth_of, above),
-        remote(up2_edge, low2_edge, edge_sem, 3, depth_of, above),
-    ]
-
-    @pl.when(has_above)
-    def _():
-        for copy in up_copies:
-            copy.start()
-
-    @pl.when(has_below)
-    def _():
-        for copy in up_copies:
-            copy.wait_recv()
-
-    @pl.when(lowest)
-    def _():
-        low2_ref[...] = jnp.zeros_like(low2_ref)
-        low2_edge[...] = jnp.zeros_like(low2_edge)
-
-    edge = jnp.broadcast_to(low2_edge[...], (slices, columns))
-    fields = [joined(low2_ref[...], edge), *fields]
+    fields = total_variation(fields, 2 * height_of - 2, layers_total, place, depth_total)
     fields = total_variation(fields, 2 * height_of - 1, layers_total, place, depth_total)
     out_ref[0] = fields[0][:slices]
     out_ref[1] = fields[1][:slices]
@@ -539,11 +538,10 @@
     taps = jnp.swapaxes(taps, 1, 2)
     tile = (SUBLANES, LANES)
     main = (slices, columns)
-    edge = (1, columns)
     vmem = pltpu.VMEM
     far_first = [
         vmem((depths, *tile), f32), vmem((far, NEAR, *tile), f32), vmem((NEAR, *tile), f32),
-        vmem((NEAR, *tile), f32), vmem((depths, *tile), f32),
+        vmem((NEAR, NEAR, *tile), f32), vmem((depths, *tile), f32),
     ]
     near_first = [
         vmem((depths, *tile), f32), vmem((NEAR, far, *tile), f32), vmem((far, *tile), f32),
@@ -552,11 +550,11 @@
     scratch = [
         vmem(volume.shape, f32), vmem(measured.shape, f32), vmem(taps.shape, f32),
         vmem(band_offset.shape, jnp.int32), pltpu.SMEM(angle_index.shape, jnp.int32),
-        vmem(main, f32), vmem(measured.shape, f32), vmem(volume.shape, f32),
+        vmem(main, f32), *[vmem((measured.shape[0], LANES), f32)] * 2, vmem(volume.shape, f32),
         vmem(taps.shape, f32), vmem(taps.shape, f32),
-        *far_first, *near_first, *far_first,
+        *near_first, *far_first, *far_first,
         vmem((3, *main), f32), vmem((3, *main), f32), vmem((3, *main), f32), vmem((3, *main), f32),
-        vmem(main, f32), vmem(main, f32), vmem(edge, f32), vmem(edge, f32),
+        vmem((2, *main), f32), vmem((2, *main), f32),
         pltpu.SemaphoreType.DMA((5,)),
         pltpu.SemaphoreType.DMA((4,)),
         pltpu.SemaphoreType.DMA((8,)),

time: 49.6 us -> 46.9 us (0.946)
  the two profiles are of different devices: /device:TPU:320 before, /device:TPU:7 now
where the time goes in v4:
time: 46.9 us; the launch traced here: 46.2 us
  Pallas kernels  44.7 us (95%)
  local copies, waits for them, and re-layouts  1.57 us (3%)
    pallas_call x1, Pallas kernels, per_device(): pl.pallas_call(functools.partial(kernel, heights, depths), out_shape=jax....  44.7 us
    unnamed x1, local copies, waits for them, and re-layouts  1.57 us

profile of v4, /device:TPU:7, one launch (start us, length us, event | category | flops | bytes accessed | tf_op | source)
XLA Modules:
  0.0 46.2 jit_solution(5304985701530899151)
XLA Ops:
  0.0 44.7 %shard_map.55 = f32[2,8,2048]{2,1,0:T(8,128)} custom-call(f32[2,8,2048]{2,1,0:T(8,128)} %vol_hbm.1, f32[16,2,64]{2,1,0:T(2,128)} %meas_hbm.1, f32[4,8,16]{2,1,0:T(8,128)} %bitcast.1, s32[16,32]{1,0:T(8,128)} %off_hbm.1, s32[16]{0:T(128)} %angle_hbm.1), custom_call_target="tpu_custom_call" | custom-call | tf_op jit(solution)/shard_map/pallas_call | solution.py:564
  44.7 1.6 %copy.7 = f32[2,8,2048]{2,1,0:T(8,128)} copy(f32[2,8,2048]{2,1,0:T(8,128)} %shard_map.55) | data formatting | bytes 262144

commit v5 on v4

--- a/solution.py
+++ b/solution.py
@@ -75,7 +75,7 @@
     out_ref,
     vol_ref, meas_ref, taps_ref, off_ref, angle_ref,
     halo_ref, band_ref, band_up, side_ref, taps_ahead, taps_behind,
-    part_1, got_1a, sum_1, got_1b, res_1,
+    part_1, got_1, res_1,
     part_2, got_2a, sum_2, got_2b, res_2,
     part_0, got_0a, sum_0, got_0b, res_0,
     up_ref, low_ref, down_ref, high_ref,
@@ -107,6 +107,13 @@
     def nears():
         return [lax.rem(near_of + i, NEAR) for i in range(1, NEAR)]
 
+    def everyone():
+        order = [(i, j) for i in range(far_count) for j in range(NEAR) if i or j]
+        order.sort(key=lambda ij: -min(ij[0], far_count - ij[0]) - min(ij[1], NEAR - ij[1]))
+        return [
+            lax.rem(far_of + i, far_count) * NEAR + lax.rem(near_of + j, NEAR) for i, j in order
+        ]
+
     @pl.when(has_below)
     def _():
         greet(depth_of, below)
@@ -115,11 +122,7 @@
     def _():
         greet(depth_of, above)
 
-    for far in fars():
-        greet(far * NEAR + near_of, height_of)
-    for near in nears():
-        greet(far_of * NEAR + near, height_of)
-    for depth in (ahead, behind):
+    for depth in everyone():
         greet(depth, height_of)
 
     loads = [
@@ -133,9 +136,6 @@
     ]
     for load in loads:
         load.start()
-    partners = far_count + NEAR + has_above.astype(jnp.int32) + has_below.astype(jnp.int32)
-    pl.semaphore_wait(barrier, partners)
-
     def remote(src, dst, sems, number, depth, height):
         return pltpu.make_async_remote_copy(
             src_ref=src, dst_ref=dst,
@@ -143,12 +143,7 @@
             device_id=(depth, height), device_id_type=MESH,
         )
 
-    halos = [
-        remote(vol_hbm.at[0], halo_ref, halo_sem, 0, depth_of, below),
-        remote(band_ref, band_up, halo_sem, 1, depth_of, below),
-    ]
-    pl.when(has_below)(halos[0].start)
-    for load in loads[1:]:
+    for load in loads:
         load.wait()
     band_pad = jnp.zeros((angles, LANES - meas_ref.shape[2]), jnp.float32)
 
@@ -157,7 +152,6 @@
         return jnp.where(depth_of % 2 == 1, pltpu.roll(band, LANES // 2, 1), band)
 
     band_ref[...] = band_of(0)
-    pl.when(has_below)(halos[1].start)
 
     row = lax.broadcasted_iota(jnp.int32, (angles, LANES), 0)
     lane = lax.broadcasted_iota(jnp.int32, (angles, LANES), 1)
@@ -221,13 +215,15 @@
 
     halves = angles // SUBLANES
 
-    def publish(image, band, ref):
+    def publish(image, ref):
         image = shift_rows(image, -offset)
         for tile in range(tiles):
             for half in range(halves):
                 ref[tile * halves + half] = -image[
                     half * SUBLANES : (half + 1) * SUBLANES, tile * LANES : (tile + 1) * LANES
                 ]
+
+    def measure(band, ref):
         for half in range(halves):
             place = depth_of // 2 * halves + half
             ref[place] = ref[place] + band[half * SUBLANES : (half + 1) * SUBLANES]
@@ -249,42 +245,30 @@
             parts = [a + b for a, b in zip(parts[::2], parts[1::2])]
         return parts[0]
 
-    class NearFirst:
-        def __init__(self, number, part, got_a, summed, got_b, res):
-            self.number, self.part, self.got_a = number, part, got_a
-            self.summed, self.got_b, self.res = summed, got_b, res
+    class Direct:
+        def __init__(self, number, part, got, res):
+            self.number, self.part, self.got, self.res = number, part, got, res
 
         def one(self):
-            size = far_count
-            to_near(lambda near: self.part.at[pl.ds(near * size, size)], self.got_a.at[near_of], self.number)
-            self.got_a[near_of] = self.part[pl.ds(near_of * size, size)]
+            for peer in everyone():
+                remote(
+                    self.part.at[peer], self.got.at[depth_of], ring_sem, self.number, peer, height_of
+                ).start()
+            self.got[depth_of] = self.part[depth_of]
 
         def two(self):
-            wait_for(self.got_a, NEAR - 1, self.number, True)
-            self.summed[...] = total([self.got_a[i] for i in range(NEAR)])
-            to_far(lambda far: self.summed.at[far], self.got_b.at[far_of], self.number + 1)
-            self.got_b[far_of] = self.summed[far_of]
-
-        def three(self):
-            wait_for(self.got_b, far_count - 1, self.number + 1, True)
-            place = near_of * far_count + far_of
-            self.res[place] = total([self.got_b[i] for i in range(far_count)])
-            mine = self.res.at[place]
-            to_far(lambda far: mine, mine, self.number + 2)
-
-        def four(self):
-            wait_for(self.res, far_count - 1, self.number + 2, True)
-            block = self.res.at[pl.ds(near_of * far_count, far_count)]
-            to_near(lambda near: block, block, self.number + 3)
+            wait_for(self.got, depths - 1, self.number, True)
+            self.res[depth_of] = total([self.got[i] for i in range(depths)])
+            mine = self.res.at[depth_of]
+            for peer in everyone():
+                remote(mine, mine, ring_sem, self.number + 1, peer, height_of).start()
 
         def five(self):
-            wait_for(self.res, depths - far_count, self.number + 3, True)
+            wait_for(self.res, depths - 1, self.number + 1, True)
 
         def settle(self):
-            wait_for(self.part, depths - far_count, self.number, False)
-            wait_for(self.summed, far_count - 1, self.number + 1, False)
-            wait_for(self.res, far_count - 1, self.number + 2, False)
-            wait_for(self.res, depths - far_count, self.number + 3, False)
+            wait_for(self.part, depths - 1, self.number, False)
+            wait_for(self.res, depths - 1, self.number + 1, False)
 
     class FarFirst:
         def __init__(self, number, part, got_a, summed, got_b, res):
@@ -316,33 +300,49 @@
             wait_for(self.got_b, NEAR - 1, self.number + 1, False)
             wait_for(self.res, depths - NEAR, self.number + 2, False)
 
-    row_1 = NearFirst(0, part_1, got_1a, sum_1, got_1b, res_1)
+    row_1 = Direct(0, part_1, got_1, res_1)
     row_2 = FarFirst(4, part_2, got_2a, sum_2, got_2b, res_2)
     row_0 = FarFirst(7, part_0, got_0a, sum_0, got_0b, res_0)
-    late = height_of == heights // 2 - 1
+    late = has_below & (height_of == heights // 2 - 1)
+    soon = jnp.logical_not(late)
     lowest = jnp.logical_not(has_below)
 
-    loads[0].wait()
     count = 3 * angles
     both = dot(own, spread([vol_ref[0], vol_ref[1]]))
     both = both[:count] + both[count:]
-    publish(both[:angles], band_of(1), part_1)
+    publish(both[:angles], part_1)
+    measure(band_of(1), part_1)
+
+    @pl.when(lowest)
+    def _():
+        publish(both[2 * angles :], part_0)
+        measure(band_ref[...], part_0)
+
+    partners = depths - 1 + has_above.astype(jnp.int32) + has_below.astype(jnp.int32)
+    pl.semaphore_wait(barrier, partners)
+
+    halos = [
+        remote(vol_hbm.at[0], halo_ref, halo_sem, 0, depth_of, below),
+        remote(band_ref, band_up, halo_sem, 1, depth_of, below),
+    ]
+
+    @pl.when(has_below)
+    def _():
+        for copy in halos:
+            copy.start()
+
     row_1.one()
-
-    @pl.when(lowest)
-    def _():
-        publish(both[2 * angles :], band_ref[...], part_0)
-        row_0.one()
-
+    pl.when(lowest)(row_0.one)
     pl.when(late)(row_1.two)
 
     @pl.when(has_above)
     def _():
-        for copy in halos:
-            copy.wait_recv()
+        halos[0].wait_recv()
         spilled = dot(from_halo, spread([halo_ref[...]]))
         image = both[angles : 2 * angles] + (spilled[:angles] + spilled[angles:])
-        publish(image, band_up[...], part_2)
+        publish(image, part_2)
+        halos[1].wait_recv()
+        measure(band_up[...], part_2)
 
     @pl.when(jnp.logical_not(has_above))
     def _():
@@ -362,7 +362,7 @@
     for copy in sides:
         copy.start()
 
-    pl.when(jnp.logical_not(late))(row_1.two)
+    pl.when(soon)(row_1.two)
     pl.when(lowest)(row_0.two)
     row_2.two()
     for copy in sides:
@@ -377,10 +377,8 @@
         beyond.append(factor(*[jnp.where(kept, part, 0.0) for part in pair]))
     beyond = transposed(beyond)
     offset_ahead, offset_behind = offset_of(ahead), offset_of(behind)
-    row_1.three()
     pl.when(lowest)(row_0.three)
     row_2.three()
-    row_1.four()
     row_1.five()
 
     zero_tile = jnp.zeros((angles, LANES), jnp.float32)
@@ -401,18 +399,13 @@
             whole = term if whole is None else whole + term
         return relax_step * whole[:, :columns]
 
-    def prepared(image):
-        moves = (offset, offset_ahead, offset_behind)
+    def prepared(image, moves):
         return [split_bf16(shift_rows(image, move)) for move in moves]
 
-    def backproject(one, two, layers):
-        def stacked(moves):
-            pairs = [image[move] for move in moves for image in (one, two)]
-            return jnp.concatenate([part for side in zip(*pairs) for part in side] * 2, axis=0)
-
-        update = dot(back, stacked((0,)))
-        outer = dot(beyond, stacked((1, 2)))
-        return [gathered(update, i) for i in layers], [gathered(outer, i) for i in layers]
+    def stacked(pairs):
+        return jnp.concatenate([part for side in zip(*pairs) for part in side] * 2, axis=0)
+
+    around = (offset_ahead, offset_behind)
 
     side_row = lax.broadcasted_iota(jnp.int32, (slices, columns), 0)
     outside = (side_row < 2) | (side_row >= last)
@@ -425,65 +418,93 @@
         two = jnp.where(side_row < 4, pltpu.roll(value, slices - 2, 0), pltpu.roll(value, 2, 0))
         return value, two
 
-    image_1 = prepared(image_of(res_1))
+    def mixed(one, two):
+        return stacked([one[0], two[0], one[1], two[1]])
+
+    def pieces(src, dst, places, number, height):
+        return [
+            remote(src.at[place], dst.at[place], edge_sem, number + i, depth_of, height)
+            for i, place in enumerate(places)
+        ]
+
+    whole_1 = image_of(res_1)
+    own_1, around_1 = prepared(whole_1, (offset,)), prepared(whole_1, around)
+    zero = jnp.zeros_like(whole_1).astype(jnp.bfloat16)
+    nothing = [(zero, zero)] * 2
+    volume_side = jnp.where(outside, side_ref[...], 0.0)
+    update = dot(back[:first], stacked([own_1[0], nothing[0]]))
+    layer_0 = vol_ref[0] + gathered(update, 0)
+    update = dot(beyond[:first], mixed(around_1, nothing))
+    side_0 = volume_side[0] + gathered(update, 0)
+    down_ref[0] = layer_0
+    down_ref[1] = side_0
+    edges = (pl.ds(0, 2), pl.ds(last, 2))
+    down_copies = pieces(
+        down_ref, high_ref, (0, (1, edges[0]), (1, edges[1]), 2, (3, edges[1])), 2, below
+    )
+    up_copies = pieces(up_ref, low_ref, (pl.ds(0, 2), 2), 0, above)
+    next_copies = pieces(up2_ref, low2_ref, (0, (1, edges[0])), 7, above)
+
+    @pl.when(has_below)
+    def _():
+        for copy in down_copies[:3]:
+            copy.start()
+
+    def completed():
+        @pl.when(has_below)
+        def _():
+            for copy in up_copies:
+                copy.wait_recv()
+
+        up2_ref[0] = layer_0 + low_ref[0]
+        up2_ref[1] = side_0 + unpacked(low_ref[2])[0]
+
+        @pl.when(has_above)
+        def _():
+            for copy in next_copies:
+                copy.start()
+
+    pl.when(late)(completed)
     row_2.five()
-    main, side = backproject(image_1, prepared(image_of(res_2)), range(3))
-    volume_side = jnp.where(outside, side_ref[...], 0.0)
-    layer_0, layer_1 = vol_ref[0] + main[0], vol_ref[1] + main[1]
-    side_0, side_1 = volume_side[0] + side[0], volume_side[1] + side[1]
-    up_ref[0] = main[2]
+    whole_2 = image_of(res_2)
+    update = dot(back[first:], stacked(own_1 + prepared(whole_2, (offset,))))
+    layer_1, part_2h2 = vol_ref[1] + gathered(update, 0), gathered(update, 1)
+    up_ref[0] = part_2h2
     up_ref[1] = layer_1
-    up_ref[2] = packed(side[2], side_1)
-    down_ref[0] = layer_0
-    down_ref[1] = layer_1
-    down_ref[2] = packed(side_0, side_1)
-    up_copy = remote(up_ref, low_ref, edge_sem, 0, depth_of, above)
-    down_copy = remote(down_ref, high_ref, edge_sem, 1, depth_of, below)
+    down_ref[2] = layer_1
+    pl.when(has_above)(up_copies[0].start)
+    pl.when(has_below)(down_copies[3].start)
+    update = dot(beyond[first:], mixed(around_1, prepared(whole_2, around)))
+    side_1, side_2h2 = volume_side[1] + gathered(update, 0), gathered(update, 1)
+    up_ref[2] = packed(side_2h2, side_1)
+    down_ref[3] = side_1
+    pl.when(has_above)(up_copies[1].start)
+    pl.when(has_below)(down_copies[4].start)
+
+    @pl.when(lowest)
+    def _():
+        row_0.five()
+        image = prepared(image_of(res_0), (offset, *around))
+        update = dot(back, stacked([nothing[0], image[0]]))
+        low_ref[0] = gathered(update, 2)
+        low_ref[1] = jnp.zeros((slices, columns), jnp.float32)
+        update = dot(beyond, mixed(nothing, image[1:]))
+        low_ref[2] = packed(gathered(update, 2), jnp.zeros((slices, columns), jnp.float32))
+
+    pl.when(soon)(completed)
 
     @pl.when(has_above)
     def _():
-        up_copy.start()
+        for copy in down_copies:
+            copy.wait_recv()
+
+    @pl.when(jnp.logical_not(has_above))
+    def _():
+        high_ref[...] = jnp.zeros_like(high_ref)
 
     @pl.when(has_below)
     def _():
-        down_copy.start()
-
-    @pl.when(lowest)
-    def _():
-        row_0.five()
-        image = prepared(image_of(res_0))
-        nothing = [[jnp.zeros_like(part) for part in pair] for pair in image]
-        low_main, low_side = backproject(nothing, image, (2,))
-        low_ref[0] = low_main[0]
-        low_ref[1] = jnp.zeros((slices, columns), jnp.float32)
-        low_ref[2] = packed(low_side[0], jnp.zeros((slices, columns), jnp.float32))
-
-    pl.when(has_below)(up_copy.wait_recv)
-    from_low, under = unpacked(low_ref[2])
-    layer_0 = layer_0 + low_ref[0]
-    side_0 = side_0 + from_low
-    up2_ref[0] = layer_0
-    up2_ref[1] = side_0
-    up_copies = [
-        remote(up2_ref.at[0], low2_ref.at[0], edge_sem, 2, depth_of, above),
-        remote(
-            up2_ref.at[1, pl.ds(0, 2)], low2_ref.at[1, pl.ds(0, 2)], edge_sem, 3, depth_of, above
-        ),
-    ]
-
-    @pl.when(has_above)
-    def _():
-        for copy in up_copies:
-            copy.start()
-        down_copy.wait_recv()
-
-    @pl.when(jnp.logical_not(has_above))
-    def _():
-        high_ref[...] = jnp.zeros_like(high_ref)
-
-    @pl.when(has_below)
-    def _():
-        for copy in up_copies:
+        for copy in next_copies:
             copy.wait_recv()
 
     @pl.when(lowest)
@@ -493,14 +514,13 @@
     def joined(inner, outer):
         return jnp.concatenate([inner, outer], axis=0)
 
-    over, over_2 = unpacked(high_ref[2])
     fields = [
         joined(low2_ref[0], jnp.where(side_row < 2, low2_ref[1], 0.0)),
-        joined(low_ref[1], under),
-        joined(layer_0, side_0),
+        joined(low_ref[1], unpacked(low_ref[2])[1]),
+        joined(up2_ref[0], up2_ref[1]),
         joined(layer_1, side_1),
-        joined(high_ref[0] + main[2], over + side[2]),
-        joined(high_ref[1], over_2),
+        joined(high_ref[0] + part_2h2, jnp.where(outside, high_ref[1], 0.0) + side_2h2),
+        joined(high_ref[2], jnp.where(side_row >= last, high_ref[3], 0.0)),
     ]
     place = lax.broadcasted_iota(jnp.int32, fields[0].shape, 0)
     place = depth_of * slices + jnp.where(place < slices + 4, place, place - 2 * slices)
@@ -518,14 +538,12 @@
 
     @pl.when(has_below)
     def _():
-        for copy in halos:
+        for copy in (*halos, *down_copies):
             copy.wait_send()
-        down_copy.wait_send()
 
     @pl.when(has_above)
     def _():
-        up_copy.wait_send()
-        for copy in up_copies:
+        for copy in (*up_copies, *next_copies):
             copy.wait_send()
 
 
@@ -543,23 +561,19 @@
         vmem((depths, *tile), f32), vmem((far, NEAR, *tile), f32), vmem((NEAR, *tile), f32),
         vmem((NEAR, NEAR, *tile), f32), vmem((depths, *tile), f32),
     ]
-    near_first = [
-        vmem((depths, *tile), f32), vmem((NEAR, far, *tile), f32), vmem((far, *tile), f32),
-        vmem((far, *tile), f32), vmem((depths, *tile), f32),
-    ]
     scratch = [
         vmem(volume.shape, f32), vmem(measured.shape, f32), vmem(taps.shape, f32),
         vmem(band_offset.shape, jnp.int32), pltpu.SMEM(angle_index.shape, jnp.int32),
         vmem(main, f32), *[vmem((measured.shape[0], LANES), f32)] * 2, vmem(volume.shape, f32),
         vmem(taps.shape, f32), vmem(taps.shape, f32),
-        *near_first, *far_first, *far_first,
-        vmem((3, *main), f32), vmem((3, *main), f32), vmem((3, *main), f32), vmem((3, *main), f32),
+        *[vmem((depths, *tile), f32)] * 3, *far_first, *far_first,
+        vmem((3, *main), f32), vmem((3, *main), f32), vmem((4, *main), f32), vmem((4, *main), f32),
         vmem((2, *main), f32), vmem((2, *main), f32),
         pltpu.SemaphoreType.DMA((5,)),
         pltpu.SemaphoreType.DMA((4,)),
         pltpu.SemaphoreType.DMA((8,)),
-        pltpu.SemaphoreType.DMA((24,)),
-        pltpu.SemaphoreType.DMA((8,)),
+        pltpu.SemaphoreType.DMA((20,)),
+        pltpu.SemaphoreType.DMA((18,)),
     ]
     return pl.pallas_call(
         functools.partial(kernel, heights, depths),

time: 46.9 us -> 43.2 us (0.921)
  the two profiles are of different devices: /device:TPU:7 before, /device:TPU:385 now
where the time goes in v5:
time: 43.2 us; the launch traced here: 43 us
  Pallas kernels  41.4 us (96%)
  local copies, waits for them, and re-layouts  1.57 us (4%)
    pallas_call x1, Pallas kernels, per_device(): pl.pallas_call(functools.partial(kernel, heights, depths), out_shape=jax....  41.4 us
    unnamed x1, local copies, waits for them, and re-layouts  1.57 us

profile of v5, /device:TPU:385, one launch (start us, length us, event | category | flops | bytes accessed | tf_op | source)
XLA Modules:
  0.0 43.0 jit_solution(6182449338388233879)
XLA Ops:
  0.0 41.4 %shard_map.55 = f32[2,8,2048]{2,1,0:T(8,128)} custom-call(f32[2,8,2048]{2,1,0:T(8,128)} %vol_hbm.1, f32[16,2,64]{2,1,0:T(2,128)} %meas_hbm.1, f32[4,8,16]{2,1,0:T(8,128)} %bitcast.1, s32[16,32]{1,0:T(8,128)} %off_hbm.1, s32[16]{0:T(128)} %angle_hbm.1), custom_call_target="tpu_custom_call" | custom-call | tf_op jit(solution)/shard_map/pallas_call | solution.py:578
  41.4 1.6 %copy.7 = f32[2,8,2048]{2,1,0:T(8,128)} copy(f32[2,8,2048]{2,1,0:T(8,128)} %shard_map.55) | data formatting | bytes 262144

commit v6 on v5

--- a/solution.py
+++ b/solution.py
@@ -44,29 +44,21 @@
     return value
 
 
-def total_variation(fields, first_layer, height_total, depth_place, depth_total):
-    rows, columns = fields[0].shape
-    lane = lax.broadcasted_iota(jnp.int32, (rows, columns), 1)
-    inner = lane < columns - 1
+def directions(here, over, layer, height_total, depth_place, depth_total):
+    rows, columns = here.shape
+    inner = lax.broadcasted_iota(jnp.int32, (rows, columns), 1) < columns - 1
     open_row = (depth_place >= 0) & (depth_place + 1 < depth_total)
-    results = []
-    under = None
-    for i in range(len(fields) - 1):
-        here = fields[i]
-        layer = first_layer + i
-        up = fields[i + 1] - here
-        up = jnp.where((layer >= 0) & (layer + 1 < height_total), up, 0.0)
-        deep = jnp.where(open_row, pltpu.roll(here, rows - 1, 0) - here, 0.0)
-        wide = jnp.where(inner, roll_left(here, 1) - here, 0.0)
-        scale = lax.rsqrt(tv_eps * tv_eps + up * up + deep * deep + wide * wide)
-        up = up * scale
-        if i:
-            deep = deep * scale
-            wide = wide * scale
-            diverge = (up - under) + (deep - pltpu.roll(deep, 1, 0)) + (wide - pltpu.roll(wide, 1, 1))
-            results.append(here + tv_step * diverge)
-        under = up
-    return results
+    up = jnp.where((layer >= 0) & (layer + 1 < height_total), over - here, 0.0)
+    deep = jnp.where(open_row, pltpu.roll(here, rows - 1, 0) - here, 0.0)
+    wide = jnp.where(inner, roll_left(here, 1) - here, 0.0)
+    scale = lax.rsqrt(tv_eps * tv_eps + up * up + deep * deep + wide * wide)
+    return up * scale, deep * scale, wide * scale
+
+
+def denoised(here, normal, under):
+    up, deep, wide = normal
+    diverge = (up - under) + (deep - pltpu.roll(deep, 1, 0)) + (wide - pltpu.roll(wide, 1, 1))
+    return here + tv_step * diverge
 
 
 def kernel(
@@ -410,14 +402,6 @@
     side_row = lax.broadcasted_iota(jnp.int32, (slices, columns), 0)
     outside = (side_row < 2) | (side_row >= last)
 
-    def packed(one, two):
-        two = jnp.where(side_row < 4, pltpu.roll(two, 2, 0), pltpu.roll(two, slices - 2, 0))
-        return jnp.where(outside, one, two)
-
-    def unpacked(value):
-        two = jnp.where(side_row < 4, pltpu.roll(value, slices - 2, 0), pltpu.roll(value, 2, 0))
-        return value, two
-
     def mixed(one, two):
         return stacked([one[0], two[0], one[1], two[1]])
 
@@ -442,8 +426,10 @@
     down_copies = pieces(
         down_ref, high_ref, (0, (1, edges[0]), (1, edges[1]), 2, (3, edges[1])), 2, below
     )
-    up_copies = pieces(up_ref, low_ref, (pl.ds(0, 2), 2), 0, above)
-    next_copies = pieces(up2_ref, low2_ref, (0, (1, edges[0])), 7, above)
+    up_copies = pieces(
+        up_ref, low_ref, (0, (1, edges[0]), (1, edges[1]), 2, (3, edges[0]), (3, edges[1])), 7, above
+    )
+    next_copies = pieces(up2_ref, low2_ref, (0, (1, edges[0])), 13, above)
 
     @pl.when(has_below)
     def _():
@@ -453,11 +439,11 @@
     def completed():
         @pl.when(has_below)
         def _():
-            for copy in up_copies:
+            for copy in up_copies[:3]:
                 copy.wait_recv()
 
         up2_ref[0] = layer_0 + low_ref[0]
-        up2_ref[1] = side_0 + unpacked(low_ref[2])[0]
+        up2_ref[1] = side_0 + jnp.where(outside, low_ref[1], 0.0)
 
         @pl.when(has_above)
         def _():
@@ -470,15 +456,21 @@
     update = dot(back[first:], stacked(own_1 + prepared(whole_2, (offset,))))
     layer_1, part_2h2 = vol_ref[1] + gathered(update, 0), gathered(update, 1)
     up_ref[0] = part_2h2
-    up_ref[1] = layer_1
+    up_ref[2] = layer_1
     down_ref[2] = layer_1
     pl.when(has_above)(up_copies[0].start)
     pl.when(has_below)(down_copies[3].start)
     update = dot(beyond[first:], mixed(around_1, prepared(whole_2, around)))
     side_1, side_2h2 = volume_side[1] + gathered(update, 0), gathered(update, 1)
-    up_ref[2] = packed(side_2h2, side_1)
+    up_ref[1] = side_2h2
+    up_ref[3] = side_1
     down_ref[3] = side_1
-    pl.when(has_above)(up_copies[1].start)
+
+    @pl.when(has_above)
+    def _():
+        for copy in up_copies[1:]:
+            copy.start()
+
     pl.when(has_below)(down_copies[4].start)
 
     @pl.when(lowest)
@@ -487,48 +479,53 @@
         image = prepared(image_of(res_0), (offset, *around))
         update = dot(back, stacked([nothing[0], image[0]]))
         low_ref[0] = gathered(update, 2)
-        low_ref[1] = jnp.zeros((slices, columns), jnp.float32)
         update = dot(beyond, mixed(nothing, image[1:]))
-        low_ref[2] = packed(gathered(update, 2), jnp.zeros((slices, columns), jnp.float32))
-
+        low_ref[1] = gathered(update, 2)
+        low_ref[2] = jnp.zeros((slices, columns), jnp.float32)
+        low_ref[3] = jnp.zeros((slices, columns), jnp.float32)
+        low2_ref[...] = jnp.zeros_like(low2_ref)
+
+    @pl.when(jnp.logical_not(has_above))
+    def _():
+        high_ref[...] = jnp.zeros_like(high_ref)
+
+    def arrive(condition, copies):
+        @pl.when(condition)
+        def _():
+            for copy in copies:
+                copy.wait_recv()
+
+    def layer_of(inner, outer, kept=outside):
+        return jnp.concatenate([inner, jnp.where(kept, outer, 0.0)], axis=0)
+
+    place = lax.broadcasted_iota(jnp.int32, (2 * slices, columns), 0)
+    place = depth_of * slices + jnp.where(place < slices + 4, place, place - 2 * slices)
+
+    def normal(here, over, layer):
+        layer = 2 * height_of + layer
+        return directions(here, over, layer, 2 * heights, place, slices * depths)
+
+    arrive(has_above, down_copies[:3])
+    at_1 = layer_of(layer_1, side_1)
+    at_2 = layer_of(high_ref[0] + part_2h2, high_ref[1] + side_2h2)
+    n_1 = normal(at_1, at_2, 1)
     pl.when(soon)(completed)
-
-    @pl.when(has_above)
-    def _():
-        for copy in down_copies:
-            copy.wait_recv()
-
-    @pl.when(jnp.logical_not(has_above))
-    def _():
-        high_ref[...] = jnp.zeros_like(high_ref)
-
-    @pl.when(has_below)
-    def _():
-        for copy in next_copies:
-            copy.wait_recv()
-
-    @pl.when(lowest)
-    def _():
-        low2_ref[...] = jnp.zeros_like(low2_ref)
-
-    def joined(inner, outer):
-        return jnp.concatenate([inner, outer], axis=0)
-
-    fields = [
-        joined(low2_ref[0], jnp.where(side_row < 2, low2_ref[1], 0.0)),
-        joined(low_ref[1], unpacked(low_ref[2])[1]),
-        joined(up2_ref[0], up2_ref[1]),
-        joined(layer_1, side_1),
-        joined(high_ref[0] + part_2h2, jnp.where(outside, high_ref[1], 0.0) + side_2h2),
-        joined(high_ref[2], jnp.where(side_row >= last, high_ref[3], 0.0)),
-    ]
-    place = lax.broadcasted_iota(jnp.int32, fields[0].shape, 0)
-    place = depth_of * slices + jnp.where(place < slices + 4, place, place - 2 * slices)
-    layers_total, depth_total = 2 * heights, slices * depths
-    fields = total_variation(fields, 2 * height_of - 2, layers_total, place, depth_total)
-    fields = total_variation(fields, 2 * height_of - 1, layers_total, place, depth_total)
-    out_ref[0] = fields[0][:slices]
-    out_ref[1] = fields[1][:slices]
+    at_0 = layer_of(up2_ref[0], up2_ref[1])
+    n_0 = normal(at_0, at_1, 0)
+    next_1 = denoised(at_1, n_1, n_0[0])
+    arrive(has_below, up_copies[3:])
+    below_1 = layer_of(low_ref[2], low_ref[3])
+    m_1 = normal(below_1, at_0, -1)
+    next_0 = denoised(at_0, n_0, m_1[0])
+    then_0 = normal(next_0, next_1, 0)
+    arrive(has_below, next_copies)
+    below_2 = layer_of(low2_ref[0], low2_ref[1], side_row < 2)
+    under_1 = denoised(below_1, m_1, normal(below_2, below_1, -2)[0])
+    out_ref[0] = denoised(next_0, then_0, normal(under_1, next_0, -1)[0])[:slices]
+    arrive(has_above, down_copies[3:])
+    at_3 = layer_of(high_ref[2], high_ref[3], side_row >= last)
+    next_2 = denoised(at_2, normal(at_2, at_3, 2), n_1[0])
+    out_ref[1] = denoised(next_1, normal(next_1, next_2, 1), then_0[0])[:slices]
 
     row_1.settle()
     row_2.settle()
@@ -567,13 +564,13 @@
         vmem(main, f32), *[vmem((measured.shape[0], LANES), f32)] * 2, vmem(volume.shape, f32),
         vmem(taps.shape, f32), vmem(taps.shape, f32),
         *[vmem((depths, *tile), f32)] * 3, *far_first, *far_first,
-        vmem((3, *main), f32), vmem((3, *main), f32), vmem((4, *main), f32), vmem((4, *main), f32),
+        *[vmem((4, *main), f32)] * 4,
         vmem((2, *main), f32), vmem((2, *main), f32),
         pltpu.SemaphoreType.DMA((5,)),
         pltpu.SemaphoreType.DMA((4,)),
         pltpu.SemaphoreType.DMA((8,)),
         pltpu.SemaphoreType.DMA((20,)),
-        pltpu.SemaphoreType.DMA((18,)),
+        pltpu.SemaphoreType.DMA((30,)),
     ]
     return pl.pallas_call(
         functools.partial(kernel, heights, depths),

time: 43.2 us -> 42.2 us (0.977)
  the two profiles are of different devices: /device:TPU:385 before, /device:TPU:7 now
where the time goes in v6:
time: 42.2 us; the launch traced here: 41.4 us
  Pallas kernels  39.8 us (94%)
  local copies, waits for them, and re-layouts  1.57 us (4%)
    pallas_call x1, Pallas kernels, per_device(): pl.pallas_call(functools.partial(kernel, heights, depths), out_shape=jax....  39.8 us
    unnamed x1, local copies, waits for them, and re-layouts  1.57 us

profile of v6, /device:TPU:7, one launch (start us, length us, event | category | flops | bytes accessed | tf_op | source)
XLA Modules:
  0.0 41.4 jit_solution(5786009481733668525)
XLA Ops:
  0.0 39.8 %shard_map.55 = f32[2,8,2048]{2,1,0:T(8,128)} custom-call(f32[2,8,2048]{2,1,0:T(8,128)} %vol_hbm.1, f32[16,2,64]{2,1,0:T(2,128)} %meas_hbm.1, f32[4,8,16]{2,1,0:T(8,128)} %bitcast.1, s32[16,32]{1,0:T(8,128)} %off_hbm.1, s32[16]{0:T(128)} %angle_hbm.1), custom_call_target="tpu_custom_call" | custom-call | tf_op jit(solution)/shard_map/pallas_call | solution.py:575
  39.8 1.6 %copy.7 = f32[2,8,2048]{2,1,0:T(8,128)} copy(f32[2,8,2048]{2,1,0:T(8,128)} %shard_map.55) | data formatting | bytes 262144

commit v7 on v6

--- a/solution.py
+++ b/solution.py
@@ -71,7 +71,7 @@
     part_2, got_2a, sum_2, got_2b, res_2,
     part_0, got_0a, sum_0, got_0b, res_0,
     up_ref, low_ref, down_ref, high_ref,
-    up2_ref, low2_ref,
+    up2_ref, low2_ref, result,
     load_sem, halo_sem, side_sem, ring_sem, edge_sem,
 ):
     height_of = lax.axis_index("height")
@@ -86,36 +86,6 @@
     tiles = columns // LANES
     angles = off_ref.shape[0]
     taps = taps_ref.shape[0]
-
-    barrier = pltpu.get_barrier_semaphore()
-
-    def greet(depth, height):
-        pl.semaphore_signal(barrier, inc=1, device_id=(depth, height), device_id_type=MESH)
-
-    def fars():
-        order = sorted(range(1, far_count), key=lambda i: -min(i, far_count - i))
-        return [lax.rem(far_of + i, far_count) for i in order]
-
-    def nears():
-        return [lax.rem(near_of + i, NEAR) for i in range(1, NEAR)]
-
-    def everyone():
-        order = [(i, j) for i in range(far_count) for j in range(NEAR) if i or j]
-        order.sort(key=lambda ij: -min(ij[0], far_count - ij[0]) - min(ij[1], NEAR - ij[1]))
-        return [
-            lax.rem(far_of + i, far_count) * NEAR + lax.rem(near_of + j, NEAR) for i, j in order
-        ]
-
-    @pl.when(has_below)
-    def _():
-        greet(depth_of, below)
-
-    @pl.when(has_above)
-    def _():
-        greet(depth_of, above)
-
-    for depth in everyone():
-        greet(depth, height_of)
 
     loads = [
         pltpu.make_async_copy(src, dst, load_sem.at[i])
@@ -135,16 +105,38 @@
             device_id=(depth, height), device_id_type=MESH,
         )
 
-    for load in loads:
+    barrier = pltpu.get_barrier_semaphore()
+
+    def greet(depth, height):
+        pl.semaphore_signal(barrier, inc=1, device_id=(depth, height), device_id_type=MESH)
+
+    def fars():
+        order = sorted(range(1, far_count), key=lambda i: -min(i, far_count - i))
+        return [lax.rem(far_of + i, far_count) for i in order]
+
+    def nears():
+        return [lax.rem(near_of + i, NEAR) for i in range(1, NEAR)]
+
+    def everyone():
+        order = [(i, j) for i in range(far_count) for j in range(NEAR) if i or j]
+        order.sort(key=lambda ij: -min(ij[0], far_count - ij[0]) - min(ij[1], NEAR - ij[1]))
+        return [
+            lax.rem(far_of + i, far_count) * NEAR + lax.rem(near_of + j, NEAR) for i, j in order
+        ]
+
+    @pl.when(has_below)
+    def _():
+        greet(depth_of, below)
+
+    @pl.when(has_above)
+    def _():
+        greet(depth_of, above)
+
+    for depth in everyone():
+        greet(depth, height_of)
+
+    for load in loads[1:4]:
         load.wait()
-    band_pad = jnp.zeros((angles, LANES - meas_ref.shape[2]), jnp.float32)
-
-    def band_of(r):
-        band = jnp.concatenate([meas_ref[:, r, :], band_pad], axis=1)
-        return jnp.where(depth_of % 2 == 1, pltpu.roll(band, LANES // 2, 1), band)
-
-    band_ref[...] = band_of(0)
-
     row = lax.broadcasted_iota(jnp.int32, (angles, LANES), 0)
     lane = lax.broadcasted_iota(jnp.int32, (angles, LANES), 1)
     view = jnp.zeros((angles, LANES), jnp.float32)
@@ -300,9 +292,18 @@
     lowest = jnp.logical_not(has_below)
 
     count = 3 * angles
+    loads[0].wait()
     both = dot(own, spread([vol_ref[0], vol_ref[1]]))
     both = both[:count] + both[count:]
     publish(both[:angles], part_1)
+    loads[4].wait()
+    band_pad = jnp.zeros((angles, LANES - meas_ref.shape[2]), jnp.float32)
+
+    def band_of(r):
+        band = jnp.concatenate([meas_ref[:, r, :], band_pad], axis=1)
+        return jnp.where(depth_of % 2 == 1, pltpu.roll(band, LANES // 2, 1), band)
+
+    band_ref[...] = band_of(0)
     measure(band_of(1), part_1)
 
     @pl.when(lowest)
@@ -518,15 +519,6 @@
     m_1 = normal(below_1, at_0, -1)
     next_0 = denoised(at_0, n_0, m_1[0])
     then_0 = normal(next_0, next_1, 0)
-    arrive(has_below, next_copies)
-    below_2 = layer_of(low2_ref[0], low2_ref[1], side_row < 2)
-    under_1 = denoised(below_1, m_1, normal(below_2, below_1, -2)[0])
-    out_ref[0] = denoised(next_0, then_0, normal(under_1, next_0, -1)[0])[:slices]
-    arrive(has_above, down_copies[3:])
-    at_3 = layer_of(high_ref[2], high_ref[3], side_row >= last)
-    next_2 = denoised(at_2, normal(at_2, at_3, 2), n_1[0])
-    out_ref[1] = denoised(next_1, normal(next_1, next_2, 1), then_0[0])[:slices]
-
     row_1.settle()
     row_2.settle()
     pl.when(lowest)(row_0.settle)
@@ -535,8 +527,28 @@
 
     @pl.when(has_below)
     def _():
-        for copy in (*halos, *down_copies):
+        for copy in (*halos, *down_copies[:3]):
             copy.wait_send()
+
+    arrive(has_below, next_copies)
+    below_2 = layer_of(low2_ref[0], low2_ref[1], side_row < 2)
+    under_1 = denoised(below_1, m_1, normal(below_2, below_1, -2)[0])
+    stores = [pltpu.make_async_copy(result.at[i], out_ref.at[i], load_sem.at[i]) for i in range(2)]
+    result[0] = denoised(next_0, then_0, normal(under_1, next_0, -1)[0])[:slices]
+    stores[0].start()
+    arrive(has_above, down_copies[3:])
+    at_3 = layer_of(high_ref[2], high_ref[3], side_row >= last)
+    next_2 = denoised(at_2, normal(at_2, at_3, 2), n_1[0])
+    result[1] = denoised(next_1, normal(next_1, next_2, 1), then_0[0])[:slices]
+    stores[1].start()
+
+    for store in stores:
+        store.wait()
+
+    @pl.when(has_below)
+    def _():
+        down_copies[3].wait_send()
+        down_copies[4].wait_send()
 
     @pl.when(has_above)
     def _():
@@ -565,7 +577,7 @@
         vmem(taps.shape, f32), vmem(taps.shape, f32),
         *[vmem((depths, *tile), f32)] * 3, *far_first, *far_first,
         *[vmem((4, *main), f32)] * 4,
-        vmem((2, *main), f32), vmem((2, *main), f32),
+        vmem((2, *main), f32), vmem((2, *main), f32), vmem(volume.shape, f32),
         pltpu.SemaphoreType.DMA((5,)),
         pltpu.SemaphoreType.DMA((4,)),
         pltpu.SemaphoreType.DMA((8,)),
@@ -576,7 +588,7 @@
         functools.partial(kernel, heights, depths),
         out_shape=jax.ShapeDtypeStruct(volume.shape, f32),
         in_specs=[pl.BlockSpec(memory_space=pl.ANY)] * 5,
-        out_specs=pl.BlockSpec(memory_space=pltpu.VMEM),
+        out_specs=pl.BlockSpec(memory_space=pl.ANY),
         scratch_shapes=scratch,
         compiler_params=pltpu.CompilerParams(
             collective_id=0, has_side_effects=True, vmem_limit_bytes=60 * 1024 * 1024

time: 42.2 us -> 41.6 us (0.986); the launches traced: 41.4 us -> 41.3 us
  no operation moved by 1% of the time
where the time goes in v7:
time: 41.6 us; the launch traced here: 41.3 us
  Pallas kernels  39.7 us (95%)
  local copies, waits for them, and re-layouts  1.57 us (4%)
    pallas_call x1, Pallas kernels, per_device(): pl.pallas_call(functools.partial(kernel, heights, depths), out_shape=jax....  39.7 us
    unnamed x1, local copies, waits for them, and re-layouts  1.57 us

profile of v7, /device:TPU:7, one launch (start us, length us, event | category | flops | bytes accessed | tf_op | source)
XLA Modules:
  0.0 41.3 jit_solution(9667478092866930259)
XLA Ops:
  0.0 39.7 %shard_map.55 = f32[2,8,2048]{2,1,0:T(8,128)} custom-call(f32[2,8,2048]{2,1,0:T(8,128)} %vol_hbm.1, f32[16,2,64]{2,1,0:T(2,128)} %meas_hbm.1, f32[4,8,16]{2,1,0:T(8,128)} %bitcast.1, s32[16,32]{1,0:T(8,128)} %off_hbm.1, s32[16]{0:T(128)} %angle_hbm.1), custom_call_target="tpu_custom_call" | custom-call | tf_op jit(solution)/shard_map/pallas_call | solution.py:587
  39.7 1.6 %copy.7 = f32[2,8,2048]{2,1,0:T(8,128)} copy(f32[2,8,2048]{2,1,0:T(8,128)} %shard_map.55) | data formatting | bytes 262144

commit v8 on v7

--- a/solution.py
+++ b/solution.py
@@ -358,9 +358,11 @@
     pl.when(soon)(row_1.two)
     pl.when(lowest)(row_0.two)
     row_2.two()
+    back = transposed([factor(lower, upper)])
+    pl.when(lowest)(row_0.three)
+    row_2.three()
     for copy in sides:
         copy.wait_recv()
-    back = transposed([factor(lower, upper)])
     beyond = []
     for ref, depth, kept in (
         (taps_ahead, ahead, lane % slices < 2),
@@ -370,8 +372,6 @@
         beyond.append(factor(*[jnp.where(kept, part, 0.0) for part in pair]))
     beyond = transposed(beyond)
     offset_ahead, offset_behind = offset_of(ahead), offset_of(behind)
-    pl.when(lowest)(row_0.three)
-    row_2.three()
     row_1.five()
 
     zero_tile = jnp.zeros((angles, LANES), jnp.float32)

time: 41.6 us -> 41.6 us (level)
  no operation moved by 1% of the time
where the time goes in v8:
time: 41.6 us; the launch traced here: 41.3 us
  Pallas kernels  39.7 us (95%)
  local copies, waits for them, and re-layouts  1.57 us (4%)
    pallas_call x1, Pallas kernels, per_device(): pl.pallas_call(functools.partial(kernel, heights, depths), out_shape=jax....  39.7 us
    unnamed x1, local copies, waits for them, and re-layouts  1.57 us

profile of v8, /device:TPU:7, one launch (start us, length us, event | category | flops | bytes accessed | tf_op | source)
XLA Modules:
  0.0 41.3 jit_solution(12576851450560649409)
XLA Ops:
  0.0 39.7 %shard_map.55 = f32[2,8,2048]{2,1,0:T(8,128)} custom-call(f32[2,8,2048]{2,1,0:T(8,128)} %vol_hbm.1, f32[16,2,64]{2,1,0:T(2,128)} %meas_hbm.1, f32[4,8,16]{2,1,0:T(8,128)} %bitcast.1, s32[16,32]{1,0:T(8,128)} %off_hbm.1, s32[16]{0:T(128)} %angle_hbm.1), custom_call_target="tpu_custom_call" | custom-call | tf_op jit(solution)/shard_map/pallas_call | solution.py:587
  39.7 1.6 %copy.7 = f32[2,8,2048]{2,1,0:T(8,128)} copy(f32[2,8,2048]{2,1,0:T(8,128)} %shard_map.55) | data formatting | bytes 262144

commit v9 on v7

--- a/solution.py
+++ b/solution.py
@@ -306,11 +306,6 @@
     band_ref[...] = band_of(0)
     measure(band_of(1), part_1)
 
-    @pl.when(lowest)
-    def _():
-        publish(both[2 * angles :], part_0)
-        measure(band_ref[...], part_0)
-
     partners = depths - 1 + has_above.astype(jnp.int32) + has_below.astype(jnp.int32)
     pl.semaphore_wait(barrier, partners)
 
@@ -325,7 +320,13 @@
             copy.start()
 
     row_1.one()
-    pl.when(lowest)(row_0.one)
+
+    @pl.when(lowest)
+    def _():
+        publish(both[2 * angles :], part_0)
+        measure(band_ref[...], part_0)
+        row_0.one()
+
     pl.when(late)(row_1.two)
 
     @pl.when(has_above)

time: 41.6 us -> 41.6 us (level)
  no operation moved by 1% of the time
where the time goes in v9:
time: 41.6 us; the launch traced here: 41.3 us
  Pallas kernels  39.7 us (95%)
  local copies, waits for them, and re-layouts  1.57 us (4%)
    pallas_call x1, Pallas kernels, per_device(): pl.pallas_call(functools.partial(kernel, heights, depths), out_shape=jax....  39.7 us
    unnamed x1, local copies, waits for them, and re-layouts  1.57 us

profile of v9, /device:TPU:7, one launch (start us, length us, event | category | flops | bytes accessed | tf_op | source)
XLA Modules:
  0.0 41.3 jit_solution(242566901156656109)
XLA Ops:
  0.0 39.7 %shard_map.55 = f32[2,8,2048]{2,1,0:T(8,128)} custom-call(f32[2,8,2048]{2,1,0:T(8,128)} %vol_hbm.1, f32[16,2,64]{2,1,0:T(2,128)} %meas_hbm.1, f32[4,8,16]{2,1,0:T(8,128)} %bitcast.1, s32[16,32]{1,0:T(8,128)} %off_hbm.1, s32[16]{0:T(128)} %angle_hbm.1), custom_call_target="tpu_custom_call" | custom-call | tf_op jit(solution)/shard_map/pallas_call | solution.py:588
  39.7 1.6 %copy.7 = f32[2,8,2048]{2,1,0:T(8,128)} copy(f32[2,8,2048]{2,1,0:T(8,128)} %shard_map.55) | data formatting | bytes 262144
